TPU v7x, 32 devices: a whole 2x2x4 slice. The times are simulated.
32 devices in a mesh: ctx: 8 (over y, x, core), fsdp: 4 (over z).
Axes of the slice: x: 2, y: 2, z: 4, core: 2. Of those that a mesh axis runs over, the one named last changes fastest.
Arguments:
- layer_input: bfloat16 [4, 1024, 768], P('fsdp', 'ctx'), may hold values from -6 to 6
- cotangent: bfloat16 [4, 1024, 768], P('fsdp', 'ctx'), may hold values from -6 to 6
- block_order: int32 [16], replicated, may hold values from 0 to 15, each once
- boundary: int32 [4], P('fsdp'), may hold values from 961 to 1023
- attn_gain: float32 [768], replicated, may hold values from 0.5 to 1.5
- attn_shift: float32 [768], replicated, may hold values from -1.5 to 1.5
- mlp_gain: float32 [768], replicated, may hold values from 0.5 to 1.5
- mlp_shift: float32 [768], replicated, may hold values from -1.5 to 1.5
- joined_weight: bfloat16 [768, 2304], P('fsdp'), may hold values from -0.3125 to 0.3125
- joined_bias: float32 [2304], replicated, may hold values from -1.5 to 1.5
- attn_weight: bfloat16 [768, 768], P(None, 'fsdp'), may hold values from -0.875 to 0.875
- attn_bias: float32 [768], replicated, may hold values from -1.5 to 1.5
- up_weight: bfloat16 [768, 3072], P('fsdp'), may hold values from -0.21875 to 0.21875
- up_bias: float32 [3072], replicated, may hold values from -1.5 to 1.5
- down_weight: bfloat16 [3072, 768], P(None, 'fsdp'), may hold values from -0.109375 to 0.109375
- down_bias: float32 [768], replicated, may hold values from -1.5 to 1.5
Outputs:
- layer_output: bfloat16 [4, 1024, 768], P('fsdp', 'ctx')
- input_grad: float32 [4, 1024, 768], P('fsdp', 'ctx')
- dattn_gain: float32 [768], replicated
- dattn_shift: float32 [768], replicated
- dmlp_gain: float32 [768], replicated
- dmlp_shift: float32 [768], replicated
- dfused_weight: float32 [768, 2304], P('fsdp')
- dfused_bias: float32 [2304], replicated
- dattn_weight: float32 [768, 768], P(None, 'fsdp')
- dattn_bias: float32 [768], replicated
- dup_weight: float32 [768, 3072], P('fsdp')
- dup_bias: float32 [3072], replicated
- ddown_weight: float32 [3072, 768], P(None, 'fsdp')
- ddown_bias: float32 [768], replicated
All inputs are finite; a program needn't handle non-finite values.
Results may differ from a plain program's by a relative error of at most 0.014.
The roundings to bfloat16 on the way count: a program that leaves them out, or rounds other values in their place, can miss the bound.
Values may be sent and summed in bfloat16 or wider, within the bound.
A program may use at most 192 MiB of HBM per device.

v0:
```python
import jax
import jax.numpy as jnp
from jax import lax
from jax.sharding import PartitionSpec as P

HEADS = 12
HEAD = 64
ROT = 16


epsilon = 1e-05
masked_score = -1e30
contract_rows = (((0,), (0,)), ((), ()))
contract_cols = (((1,), (1,)), ((), ()))


def place_lookup(block_order, begin, count, half):
    storage = begin + jnp.arange(count, dtype=jnp.int32)
    slots = storage // half
    table = jnp.arange(block_order.shape[0], dtype=jnp.int32)
    chosen = jnp.sum(jnp.where(slots[:, None] == table[None, :], block_order[None, :], 0), axis=1)
    return chosen * half + storage % half


def normalize_parts(value):
    average = jnp.mean(value, -1, keepdims=True)
    centered = value - average
    inverse = lax.rsqrt(jnp.mean(centered * centered, -1, keepdims=True) + epsilon)
    return (centered * inverse, inverse)


def norm_back(d_norm, normal, inverse, gain):
    scaled = d_norm * gain
    inner = (
        scaled
        - jnp.mean(scaled, -1, keepdims=True)
        - normal * jnp.mean(scaled * normal, -1, keepdims=True)
    )
    return (inner * inverse, jnp.sum(d_norm * normal, 0), jnp.sum(d_norm, 0))


def rotary_tables(places):
    half = ROT // 2
    freq = 10000.0 ** (-2.0 * jnp.arange(half, dtype=jnp.float32) / ROT)
    angles = places.astype(jnp.float32)[:, None] * freq[None, :]
    return (jnp.cos(angles)[:, None, :], jnp.sin(angles)[:, None, :])


def rotate(tensor, cosine, sine):
    half = ROT // 2
    first = tensor[..., :half]
    second = tensor[..., half:ROT]
    return jnp.concatenate(
        [first * cosine - second * sine, second * cosine + first * sine, tensor[..., ROT:]], -1
    )


def rotate_back(tensor, cosine, sine):
    half = ROT // 2
    first = tensor[..., :half]
    second = tensor[..., half:ROT]
    return jnp.concatenate(
        [first * cosine + second * sine, second * cosine - first * sine, tensor[..., ROT:]], -1
    )


def pair_terms(
    query_heads,
    query_pl,
    query_dc,
    mix_grad,
    log_total,
    delta_rows,
    key_heads,
    value_heads,
    key_pl,
    key_dc,
    scale,
):
    scores = (
        jnp.einsum("qhd,khd->hqk", query_heads, key_heads, preferred_element_type=jnp.float32)
        * scale
    )
    valid = ((key_pl[None, :] <= query_pl[:, None]) & (key_dc[None, :] == query_dc[:, None]))[None]
    scores = jnp.where(valid, scores, masked_score)
    prob = jnp.where(valid, jnp.exp(scores - log_total[..., None]), 0.0)
    d_prob = jnp.einsum("qhd,khd->hqk", mix_grad, value_heads, preferred_element_type=jnp.float32)
    d_score = (prob * (d_prob - delta_rows[..., None])).astype(jnp.bfloat16)
    return (prob, d_score)


def local(
    layer_input,
    cotangent,
    block_order,
    boundary,
    attn_gain,
    attn_shift,
    mlp_gain,
    mlp_shift,
    joined_weight,
    joined_bias,
    attn_weight,
    attn_bias,
    up_weight,
    up_bias,
    down_weight,
    down_bias,
):
    local_rows = layer_input.shape[1]
    width = layer_input.shape[2]
    context = lax.axis_size("ctx")
    length = local_rows * context
    half = local_rows // 2
    blocks = 2 * context
    key_tile = min(512, length)
    tiles_all = length // key_tile
    scale = HEAD ** (-0.5)
    cutoff = boundary[0]
    hidden = layer_input[0].astype(jnp.float32)
    grad_out = cotangent[0]
    my_index = lax.axis_index("ctx")
    begin = my_index * local_rows
    query_places = place_lookup(block_order, begin, local_rows, half)
    query_docs = (query_places >= cutoff).astype(jnp.int32)
    cosine, sine = rotary_tables(query_places)
    table = jnp.arange(blocks, dtype=jnp.int32)
    inverse_order = jnp.sum(
        jnp.where(block_order[None, :] == table[:, None], table[None, :], 0), axis=1
    )

    def place_order(whole):
        columns = whole.shape[1]
        return jnp.take(whole.reshape(blocks, half, columns), inverse_order, axis=0).reshape(
            length, columns
        )

    def block_first(index):
        return lax.dynamic_index_in_dim(block_order, 2 * my_index + index, 0, keepdims=False) * half

    normal, inverse = normalize_parts(hidden)
    norm_attn = (normal * attn_gain + attn_shift).astype(jnp.bfloat16)
    norm_mlp = (normal * mlp_gain + mlp_shift).astype(jnp.bfloat16)
    joined_full, up_full = (
        lax.all_gather(joined_weight, "fsdp", axis=0, tiled=True),
        lax.all_gather(up_weight, "fsdp", axis=0, tiled=True),
    )
    attn_full, down_full = (
        lax.all_gather(attn_weight, "fsdp", axis=1, tiled=True),
        lax.all_gather(down_weight, "fsdp", axis=1, tiled=True),
    )
    joined_lin = jnp.dot(norm_attn, joined_full, preferred_element_type=jnp.float32)
    up_lin = jnp.dot(norm_mlp, up_full, preferred_element_type=jnp.float32)
    joined = joined_lin + joined_bias
    queries = (
        rotate(joined[:, :width].reshape(local_rows, HEADS, HEAD), cosine, sine)
        .astype(jnp.bfloat16)
        .reshape(local_rows, width)
    )
    keys = (
        rotate(joined[:, width : 2 * width].reshape(local_rows, HEADS, HEAD), cosine, sine)
        .astype(jnp.bfloat16)
        .reshape(local_rows, width)
    )
    values = joined[:, 2 * width :].astype(jnp.bfloat16)
    kv_whole = lax.all_gather(jnp.concatenate([keys, values], 1), "ctx", axis=0, tiled=True)
    kv_ordered = place_order(kv_whole)

    def key_block_at(index):
        start = index * key_tile
        block = lax.dynamic_slice_in_dim(kv_ordered, start, key_tile, 0)
        key_pl = start + jnp.arange(key_tile, dtype=jnp.int32)
        key_dc = (key_pl >= cutoff).astype(jnp.int32)
        return (
            block[:, :width].reshape(key_tile, HEADS, HEAD),
            block[:, width:].reshape(key_tile, HEADS, HEAD),
            key_pl,
            key_dc,
        )

    mixtures = []
    tops = []
    totals = []
    for part in range(2):
        q_heads = queries[part * half : (part + 1) * half].reshape(half, HEADS, HEAD)
        q_pl = query_places[part * half : (part + 1) * half]
        q_dc = query_docs[part * half : (part + 1) * half]
        reach = (block_first(part) + half + key_tile - 1) // key_tile

        def forward_step(index, state, q_heads=q_heads, q_pl=q_pl, q_dc=q_dc):
            mixture, top, total = state
            key_heads, value_heads, key_pl, key_dc = key_block_at(index)
            scores = (
                jnp.einsum("qhd,khd->hqk", q_heads, key_heads, preferred_element_type=jnp.float32)
                * scale
            )
            valid = ((key_pl[None, :] <= q_pl[:, None]) & (key_dc[None, :] == q_dc[:, None]))[None]
            scores = jnp.where(valid, scores, masked_score)
            new_top = jnp.maximum(top, jnp.max(scores, -1))
            weights = jnp.where(valid, jnp.exp(scores - new_top[..., None]), 0.0)
            factor = jnp.exp(top - new_top)
            total = total * factor + jnp.sum(weights, -1)
            mixture = mixture * factor.T[:, :, None] + jnp.einsum(
                "hqk,khd->qhd",
                weights.astype(jnp.bfloat16),
                value_heads,
                preferred_element_type=jnp.float32,
            )
            return (mixture, new_top, total)

        start_state = (
            jnp.zeros((half, HEADS, HEAD), jnp.float32),
            jnp.full((HEADS, half), masked_score, jnp.float32),
            jnp.zeros((HEADS, half), jnp.float32),
        )
        mixture, top, total = lax.fori_loop(jnp.int32(0), reach, forward_step, start_state)
        mixtures.append(mixture)
        tops.append(top)
        totals.append(total)
    mixture = jnp.concatenate(mixtures, 0)
    top = jnp.concatenate(tops, 1)
    total = jnp.concatenate(totals, 1)
    logsum = top + jnp.log(total)
    mixed = mixture / total.T[:, :, None]
    mix_low = mixed.reshape(local_rows, width).astype(jnp.bfloat16)
    upper = up_lin + up_bias
    act, gelu_pull = jax.vjp(lambda argument: jax.nn.gelu(argument, approximate=False), upper)
    act_low = act.astype(jnp.bfloat16)
    branches = jnp.dot(mix_low, attn_full, preferred_element_type=jnp.float32) + jnp.dot(
        act_low, down_full, preferred_element_type=jnp.float32
    )
    layer_output = (hidden + branches + attn_bias + down_bias).astype(jnp.bfloat16)
    d_attn = lax.dot_general(grad_out, attn_full, contract_cols, preferred_element_type=jnp.float32)
    d_act = lax.dot_general(grad_out, down_full, contract_cols, preferred_element_type=jnp.float32)
    d_mix_flat = d_attn.astype(jnp.bfloat16)
    d_mix = d_mix_flat.reshape(local_rows, HEADS, HEAD)
    delta = jnp.einsum("qhd,qhd->hq", d_mix.astype(jnp.float32), mixed)
    d_up = gelu_pull(d_act)[0]
    d_up_low = d_up.astype(jnp.bfloat16)
    query_grads = []
    for part in range(2):
        q_heads = queries[part * half : (part + 1) * half].reshape(half, HEADS, HEAD)
        q_pl = query_places[part * half : (part + 1) * half]
        q_dc = query_docs[part * half : (part + 1) * half]
        g_heads = d_mix[part * half : (part + 1) * half]
        log_rows = logsum[:, part * half : (part + 1) * half]
        delta_part = delta[:, part * half : (part + 1) * half]
        reach = (block_first(part) + half + key_tile - 1) // key_tile

        def query_step(
            index,
            d_query,
            q_heads=q_heads,
            q_pl=q_pl,
            q_dc=q_dc,
            g_heads=g_heads,
            log_rows=log_rows,
            delta_part=delta_part,
        ):
            key_heads, value_heads, key_pl, key_dc = key_block_at(index)
            prob, d_score = pair_terms(
                q_heads,
                q_pl,
                q_dc,
                g_heads,
                log_rows,
                delta_part,
                key_heads,
                value_heads,
                key_pl,
                key_dc,
                scale,
            )
            return (
                d_query
                + jnp.einsum("hqk,khd->qhd", d_score, key_heads, preferred_element_type=jnp.float32)
                * scale
            )

        query_grads.append(
            lax.fori_loop(
                jnp.int32(0), reach, query_step, jnp.zeros((half, HEADS, HEAD), jnp.float32)
            )
        )
    d_query = jnp.concatenate(query_grads, 0)
    packed_whole = lax.all_gather(
        jnp.concatenate([queries, d_mix_flat], 1), "ctx", axis=0, tiled=True
    )
    stats_whole = lax.all_gather(jnp.concatenate([logsum.T, delta.T], 1), "ctx", axis=0, tiled=True)
    packed_ordered = place_order(packed_whole)
    stats_ordered = place_order(stats_whole)
    key_grads = []
    value_grads = []
    for part in range(2):
        own_keys = keys[part * half : (part + 1) * half].reshape(half, HEADS, HEAD)
        own_values = values[part * half : (part + 1) * half].reshape(half, HEADS, HEAD)
        own_pl = query_places[part * half : (part + 1) * half]
        own_dc = query_docs[part * half : (part + 1) * half]
        first_tile = block_first(part) // key_tile

        def owner_step(
            index, state, own_keys=own_keys, own_values=own_values, own_pl=own_pl, own_dc=own_dc
        ):
            start = index * key_tile
            block = lax.dynamic_slice_in_dim(packed_ordered, start, key_tile, 0)
            stat_block = lax.dynamic_slice_in_dim(stats_ordered, start, key_tile, 0)
            q_heads = block[:, :width].reshape(key_tile, HEADS, HEAD)
            g_heads = block[:, width:].reshape(key_tile, HEADS, HEAD)
            q_pl = start + jnp.arange(key_tile, dtype=jnp.int32)
            q_dc = (q_pl >= cutoff).astype(jnp.int32)
            prob, d_score = pair_terms(
                q_heads,
                q_pl,
                q_dc,
                g_heads,
                stat_block[:, :HEADS].T,
                stat_block[:, HEADS:].T,
                own_keys,
                own_values,
                own_pl,
                own_dc,
                scale,
            )
            d_key = (
                jnp.einsum("hqk,qhd->khd", d_score, q_heads, preferred_element_type=jnp.float32)
                * scale
            )
            d_value = jnp.einsum(
                "hqk,qhd->khd",
                prob.astype(jnp.bfloat16),
                g_heads,
                preferred_element_type=jnp.float32,
            )
            return (state[0] + d_key, state[1] + d_value)

        zero_heads = jnp.zeros((half, HEADS, HEAD), jnp.float32)
        part_key, part_value = lax.fori_loop(
            first_tile, jnp.int32(tiles_all), owner_step, (zero_heads, zero_heads)
        )
        key_grads.append(part_key)
        value_grads.append(part_value)
    key_grad_heads = jnp.concatenate(key_grads, 0)
    value_grad_rows = jnp.concatenate(value_grads, 0).reshape(local_rows, width)
    d_joined = jnp.concatenate(
        [
            rotate_back(d_query, cosine, sine).reshape(local_rows, width),
            rotate_back(key_grad_heads, cosine, sine).reshape(local_rows, width),
            value_grad_rows,
        ],
        1,
    )
    d_joined_low = d_joined.astype(jnp.bfloat16)
    d_norm_attn = lax.dot_general(
        d_joined_low, joined_full, contract_cols, preferred_element_type=jnp.float32
    )
    d_norm_mlp = lax.dot_general(
        d_up_low, up_full, contract_cols, preferred_element_type=jnp.float32
    )
    back_attn, gain_attn, shift_attn = norm_back(d_norm_attn, normal, inverse, attn_gain)
    back_mlp, gain_mlp, shift_mlp = norm_back(d_norm_mlp, normal, inverse, mlp_gain)
    input_grad = grad_out.astype(jnp.float32) + back_attn + back_mlp
    shard_rows = joined_weight.shape[0]
    shard_begin = lax.axis_index("fsdp") * shard_rows
    n_attn = lax.all_gather(norm_attn, "fsdp", axis=0, tiled=True)
    n_mlp = lax.all_gather(norm_mlp, "fsdp", axis=0, tiled=True)
    g_joined = lax.all_gather(d_joined_low, "fsdp", axis=0, tiled=True)
    g_up = lax.all_gather(d_up_low, "fsdp", axis=0, tiled=True)
    g_out = lax.all_gather(grad_out, "fsdp", axis=0, tiled=True)
    m_low = lax.all_gather(mix_low, "fsdp", axis=0, tiled=True)
    a_low = lax.all_gather(act_low, "fsdp", axis=0, tiled=True)
    cols_attn = lax.dynamic_slice_in_dim(n_attn, shard_begin, shard_rows, 1)
    cols_mlp = lax.dynamic_slice_in_dim(n_mlp, shard_begin, shard_rows, 1)
    out_cols = lax.dynamic_slice_in_dim(g_out, shard_begin, shard_rows, 1)
    dfused_weight, dup_weight, dattn_weight, ddown_weight = (
        lax.psum(
            lax.dot_general(
                cols_attn, g_joined, contract_rows, preferred_element_type=jnp.float32
            ).astype(jnp.bfloat16),
            "ctx",
        ).astype(jnp.float32),
        lax.psum(
            lax.dot_general(
                cols_mlp, g_up, contract_rows, preferred_element_type=jnp.float32
            ).astype(jnp.bfloat16),
            "ctx",
        ).astype(jnp.float32),
        lax.psum(
            lax.dot_general(
                m_low, out_cols, contract_rows, preferred_element_type=jnp.float32
            ).astype(jnp.bfloat16),
            "ctx",
        ).astype(jnp.float32),
        lax.psum(
            lax.dot_general(
                a_low, out_cols, contract_rows, preferred_element_type=jnp.float32
            ).astype(jnp.bfloat16),
            "ctx",
        ).astype(jnp.float32),
    )
    out_sum = jnp.sum(grad_out.astype(jnp.float32), 0)
    small = lax.psum(
        (
            gain_attn,
            shift_attn,
            gain_mlp,
            shift_mlp,
            jnp.sum(d_joined, 0),
            out_sum,
            jnp.sum(d_up, 0),
        ),
        ("ctx", "fsdp"),
    )
    return (
        layer_output[None],
        input_grad[None],
        small[0],
        small[1],
        small[2],
        small[3],
        dfused_weight,
        small[4],
        dattn_weight,
        small[5],
        dup_weight,
        small[6],
        ddown_weight,
        small[5],
    )


def solution(mesh):
    return jax.shard_map(
        local,
        mesh=mesh,
        in_specs=(
            P("fsdp", "ctx", None),
            P("fsdp", "ctx", None),
            P(),
            P("fsdp"),
            P(),
            P(),
            P(),
            P(),
            P("fsdp", None),
            P(),
            P(None, "fsdp"),
            P(),
            P("fsdp", None),
            P(),
            P(None, "fsdp"),
            P(),
        ),
        out_specs=(
            P("fsdp", "ctx", None),
            P("fsdp", "ctx", None),
            P(),
            P(),
            P(),
            P(),
            P("fsdp", None),
            P(),
            P(None, "fsdp"),
            P(),
            P("fsdp", None),
            P(),
            P(None, "fsdp"),
            P(),
        ),
        check_vma=False,
    )
```

profile of v0, /device:TPU:0, one launch (start us, length us, event | category | flops | bytes accessed | tf_op | source)
XLA Modules:
  0.0 686.6 jit_solution(15322701241697512506)
XLA Ops:
  11.0 71.3 %all-gather.11.cloned.1.call-done = bf16[768,2304]{1,0:T(8,128)(2,1)} async-done(((bf16[192,2304]{1,0:T(8,128)(2,1)}), bf16[768,2304]{1,0:T(8,128)(2,1)}) %all-gather.11.cloned.1.call-update) | async-done | bytes 3538960 | tf_op jit(solution)/shard_map/all_gather | solution.py:145
  82.3 2.6 fusion.148
  86.6 26.3 %all-gather.15.cloned.1.call-done = bf16[768,768]{0,1:T(8,128)(2,1)} async-done(((bf16[768,192]{0,1:T(8,128)(2,1)}), bf16[768,768]{0,1:T(8,128)(2,1)}) %all-gather.15.cloned.1.call-update) | async-done | bytes 1179664 | tf_op jit(solution)/shard_map/all_gather | solution.py:149
  113.0 1.6 convolution_convert_fusion.4
  115.6 87.5 %all-gather.17.cloned.1.call-done = bf16[768,3072]{1,0:T(8,128)(2,1)} async-done(((bf16[192,3072]{1,0:T(8,128)(2,1)}), bf16[768,3072]{1,0:T(8,128)(2,1)}) %all-gather.17.cloned.1.call-update) | async-done | bytes 4718608 | tf_op jit(solution)/shard_map/all_gather | solution.py:146
  203.1 7.7 %multiply_convert_fusion.2 = (bf16[128,3072]{1,0:T(8,128)(2,1)}, f32[128,3072]{1,0:T(8,128)}) fusion(f32[3072]{0:T(1024)S(1)} %copy-done.68, bf16[128,768]{1,0:T(8,128)(2,1)S(1)} %get-tuple-element.755, bf16[768,3072]{1,0:T(8,128)(2,1)} %all-gather.17.cloned.1.call-done), kind=kOutput, calls=%fused_computation.125 | convolution fusion | flops 629932032 | bytes 7286784 | tf_op jit(solution)/shard_map/dot_general | solution.py:153
  223.8 68.6 %all-gather.19.cloned.1.call-done = bf16[3072,768]{0,1:T(8,128)(2,1)} async-done(((bf16[3072,192]{0,1:T(8,128)(2,1)}), bf16[3072,768]{0,1:T(8,128)(2,1)}) %all-gather.19.cloned.1.call-update) | async-done | bytes 4718608 | tf_op jit(solution)/shard_map/all_gather | solution.py:150
  292.4 8.1 %fusion.137 = (f32[3072]{0:T(1024)}, bf16[128,3072]{1,0:T(8,128)(2,1)}) fusion(f32[128,3072]{1,0:T(8,128)S(1)} %copy-done.69, bf16[3072,768]{0,1:T(8,128)(2,1)} %all-gather.19.cloned.1.call-done, bf16[1,128,768]{2,1,0:T(8,128)(2,1)S(1)} %copy-done.19), kind=kOutput, calls=%fused_computation.262 | convolution fusion | flops 632681472 | bytes 7286784 | tf_op jit(solution)/shard_map/dot_general | solution.py:234
  300.6 24.9 %all-gather.13.cloned.1.call-done = bf16[1024,1536]{1,0:T(8,128)(2,1)} async-done(((bf16[128,1536]{1,0:T(8,128)(2,1)}), bf16[1024,1536]{1,0:T(8,128)(2,1)}) %all-gather.13.cloned.1.call-update) | async-done | bytes 3145744 | tf_op jit(solution)/shard_map/all_gather | solution.py:166
  325.5 2.6 gather_fusion.1
  328.2 32.0 %all-gather.21.cloned.1.call-done = bf16[1024,1536]{1,0:T(8,128)(2,1)} async-done(((bf16[128,1536]{1,0:T(8,128)(2,1)}), bf16[1024,1536]{1,0:T(8,128)(2,1)}) %all-gather.21.cloned.1.call-update) | async-done | bytes 3145744 | tf_op jit(solution)/shard_map/all_gather | solution.py:286
  360.2 4.3 gather_fusion.2
  364.6 5.3 broadcast_select_fusion
  369.8 3.2 copy.87
  373.7 5.2 while.72
  380.3 2.6 while.73
  383.7 1.2 fusion.110
  387.1 17.6 %while.74 = (s32[]{:T(128)}, f32[64,12,64]{0,2,1:T(8,128)}, s32[]{:T(128)}, bf16[1024,1536]{0,1:T(8,128)(2,1)S(1)}, s32[64]{0:T(128)}, /*index=5*/s32[]{:T(128)}...) while((s32[]{:T(128)}, f32[64,12,64]{0,2,1:T(8,128)}, ...), condition=%wide.region_13.15_spmd, body=%wide.region_12.14_spmd.sunk | while | flops 153946112 | bytes 12862291 | solution.py:281
  389.3 1.5 fusion.273
  392.2 3.9 fusion.274
  398.0 1.5 fusion.273
  400.9 3.8 fusion.274
  405.5 8.6 %while.75 = (s32[]{:T(128)}, f32[64,12,64]{0,2,1:T(8,128)}, s32[]{:T(128)}, bf16[1024,1536]{0,1:T(8,128)(2,1)S(1)}, s32[64]{0:T(128)S(1)}, /*index=5*/s32[]{:T(1...) while((s32[]{:T(128)}, f32[64,12,64]{0,2,1:T(8,128)}, ...), condition=%wide.region_15.17_spmd, body=%wide.region_14.16_spmd.sunk | while | flops 153946112 | bytes 12860187 | solution.py:281
  407.4 1.5 fusion.281
  410.3 3.8 fusion.282
  414.8 20.3 %all_gather.48 = f32[1024,24]{0,1:T(8,128)S(1)} all-gather(f32[128,24]{0,1:T(8,128)S(1)} %pad_maximum_fusion.8), channel_id=1, replica_groups=mesh['ctx'=8,'fsdp'=4] {'ctx'}, dimensions={0}, use_global_device_ids=true | all-gather | bytes 110592 | tf_op jit(solution)/shard_map/all_gather | solution.py:289
  436.1 4.6 copy.101
  443.0 9.8 %while.76 = (s32[]{:T(128)}, f32[64,12,64]{0,2,1:T(8,128)}, f32[64,12,64]{0,2,1:T(8,128)}, bf16[1024,1536]{0,1:T(8,128)(2,1)}, s32[64]{0:T(128)S(1)}, /*index=5*...) while((s32[]{:T(128)}, f32[64,12,64]{0,2,1:T(8,128)}, ...), condition=%wide.region_17.19_spmd, body=%wide.region_16.18_spmd.sunk | while | flops 204720128 | bytes 12215031 | solution.py:337
  443.0 1.5 fusion.290
  444.5 1.5 dynamic-slice_bitcast_fusion.6
  446.8 1.4 exponential_select_fusion.6
  448.2 2.1 fusion.292
  450.4 2.4 fusion.291
  452.8 1.6 multiply_add_fusion.4
  456.0 19.5 %while.77 = (s32[]{:T(128)}, f32[64,12,64]{0,2,1:T(8,128)}, f32[64,12,64]{0,2,1:T(8,128)}, bf16[1024,1536]{0,1:T(8,128)(2,1)}, s32[64]{0:T(128)S(1)}, /*index=5*...) while((s32[]{:T(128)}, f32[64,12,64]{0,2,1:T(8,128)}, ...), condition=%wide.region_19.21_spmd, body=%wide.region_18.20_spmd.sunk | while | flops 204720128 | bytes 12215031 | solution.py:337
  456.0 1.5 fusion.300
  457.5 1.5 dynamic-slice_bitcast_fusion.7
  459.8 1.4 exponential_select_fusion.7
  461.3 2.1 fusion.302
  463.4 2.4 fusion.301
  465.8 1.5 fusion.300
  467.3 1.5 dynamic-slice_bitcast_fusion.7
  469.6 1.4 exponential_select_fusion.7
  471.0 2.1 fusion.302
  473.1 2.4 fusion.301
  476.6 1.3 fusion.106
  478.1 1.3 pad_maximum_fusion.3
  480.4 22.1 %all_gather.49 = bf16[512,768]{1,0:T(8,128)(2,1)} all-gather(bf16[128,768]{1,0:T(8,128)(2,1)S(1)} %copy-done.18), channel_id=1, replica_groups=mesh['ctx'=8,'fsdp'=4] {'fsdp'}, dimensions={0}, use_global_device_ids=true | all-gather | bytes 983040 | tf_op jit(solution)/shard_map/all_gather | solution.py:364
  502.5 28.5 %all-gather = bf16[1,512,768]{2,1,0:T(8,128)(2,1)S(1)} all-gather(bf16[1,128,768]{2,1,0:T(8,128)(2,1)S(1)} %copy-done.20), channel_id=2, replica_groups=mesh['ctx'=8,'fsdp'=4] {'fsdp'}, dimensions={1}, use_global_device_ids=true | all-gather | bytes 983040 | tf_op jit(solution)/shard_map/all_gather | solution.py:368
  531.0 30.9 %all_gather.53 = bf16[512,768]{1,0:T(8,128)(2,1)} all-gather(bf16[128,768]{1,0:T(8,128)(2,1)} %copy-done.26), channel_id=1, replica_groups=mesh['ctx'=8,'fsdp'=4] {'fsdp'}, dimensions={0}, use_global_device_ids=true | all-gather | bytes 983040 | tf_op jit(solution)/shard_map/all_gather | solution.py:365
  562.0 4.9 fusion.152
  567.1 18.3 %all_gather.51 = bf16[512,768]{0,1:T(8,128)(2,1)S(1)} all-gather(bf16[128,768]{0,1:T(8,128)(2,1)S(1)} %fusion.107), channel_id=1, replica_groups=mesh['ctx'=8,'fsdp'=4] {'fsdp'}, dimensions={0}, use_global_device_ids=true | all-gather | bytes 983040 | tf_op jit(solution)/shard_map/all_gather | solution.py:369
  585.3 1.3 convolution_convert_fusion.3
  586.7 3.8 convolution_convert_fusion
  590.5 3.9 convolution_convert_fusion.1
  594.4 3.8 convolution_convert_fusion.2
  599.4 4.2 fusion.151
  604.0 1.5 fusion.102
  606.7 40.8 %all-reduce = (f32[768]{0:T(1024)}, f32[768]{0:T(1024)}, f32[768]{0:T(1024)}, f32[768]{0:T(1024)}, f32[2304]{0:T(1024)}, /*index=5*/f32[768]{0:T(1024)S(1)}, f32[3072]{0:T(1024)}) all-reduce(f32[768]{0:T(1024)S(1)} %get-tuple-element.567, f32[768]{0:T(1024)S(1)} %get-tuple-element.572, ...), channel_id=1, replica_groups=mesh['ctx'=8,'fsdp'=4] {'ctx','fsdp'}, use_global_device_ids=true, to_apply=%region_25.27 | all-reduce | flops 9216 | bytes 73728 | tf_op jit(solution)/shard_map/psum | solution.py:401
  647.5 1.2 fusion.76
  648.7 23.6 %all-reduce.4.cloned.1.call-done = (bf16[192,2304]{1,0:T(8,128)(2,1)}, bf16[768,192]{0,1:T(8,128)(2,1)}, bf16[192,3072]{1,0:T(8,128)(2,1)}, bf16[3072,192]{0,1:T(8,128)(2,1)}) async-done(((bf16[192,2304]{1,0:T(8,128)(2,1)}, bf16[768,192]{0,1:T(8,128)(2,1)}, bf16[192,3072]{1,0:T(8,128)(2,1)}, bf16[3072,192]{0,1:T(8,128)(2,1)}), (bf16[192,2304]{1,0:T(8,128)(2,1)}, bf16[768,192]{0,1:T(8,128)(2,1)}, ...) | async-done | bytes 3538960 | tf_op jit(solution)/shard_map/psum | solution.py:375
  672.3 3.0 convert_element_type.172
  675.3 1.7 convert_element_type.174
  677.0 1.3 convert_element_type.168
  (317 shorter events, 54.4 us)
Async XLA Ops:
  7.2 3.0 copy-start.67
  7.2 3.0 copy-start.10
  7.2 75.1 %all-gather.11.cloned.1.call-start = ((), (), s32[]{:S(2)}) async-start(), calls=%async_computation | async-start | bytes 4423680 | tf_op jit(solution)/shard_map/all_gather | solution.py:145
  7.9 2.8 copy-start.51
  8.0 2.8 copy-start.53
  8.0 2.8 copy-start.59
  8.0 2.8 copy-start.60
  8.0 105.0 %all-gather.15.cloned.1.call-start = ((), (), s32[]{:S(2)}) async-start(), calls=%async_computation.2 | async-start | bytes 1474560 | tf_op jit(solution)/shard_map/all_gather | solution.py:149
  8.7 73.6 %copy-start.55 = (f32[2304]{0:T(1024)S(1)}, f32[2304]{0:T(1024)}, u32[]{:S(2)}) copy-start(f32[2304]{0:T(1024)} %param.39) | copy-start | bytes 27652
  8.7 194.4 %all-gather.17.cloned.1.call-start = ((), (), s32[]{:S(2)}) async-start(), calls=%async_computation.3 | async-start | bytes 5898240 | tf_op jit(solution)/shard_map/all_gather | solution.py:146
  9.5 282.9 %all-gather.19.cloned.1.call-start = ((), (), s32[]{:S(2)}) async-start(), calls=%async_computation.4 | async-start | bytes 5898240 | tf_op jit(solution)/shard_map/all_gather | solution.py:150
  10.1 315.5 %all-gather.13.cloned.1.call-start = ((), (), s32[]{:S(2)}) async-start(), calls=%async_computation.1 | async-start | bytes 3538944 | tf_op jit(solution)/shard_map/all_gather | solution.py:166
  10.4 74.6 %copy-start.57 = (f32[128]{0:T(128)}, f32[128]{0:T(128)S(1)}, u32[]{:S(2)}) copy-start(f32[128]{0:T(128)S(1)} %broadcast_multiply_fusion.4) | copy-start | bytes 1540
  10.6 74.4 %copy-start.65 = (f32[128]{0:T(128)}, f32[128]{0:T(128)S(1)}, u32[]{:S(2)}) copy-start(f32[128]{0:T(128)S(1)} %add_rsqrt_fusion) | copy-start | bytes 1540
  10.8 74.7 %copy-start.45 = (f32[128,8]{0,1:T(8,128)}, f32[128,8]{0,1:T(8,128)S(1)}, u32[]{:S(2)}) copy-start(f32[128,8]{0,1:T(8,128)S(1)} %get-tuple-element.773) | copy-start | bytes 12292
  10.8 74.7 %copy-start.47 = (f32[128,8]{0,1:T(8,128)}, f32[128,8]{0,1:T(8,128)S(1)}, u32[]{:S(2)}) copy-start(f32[128,8]{0,1:T(8,128)S(1)} %get-tuple-element.774) | copy-start | bytes 12292
  11.0 74.0 %copy-start.17 = (bf16[128,768]{1,0:T(8,128)(2,1)}, bf16[128,768]{1,0:T(8,128)(2,1)S(1)}, u32[]{:S(2)}) copy-start(bf16[128,768]{1,0:T(8,128)(2,1)S(1)} %get-tuple-element.754) | copy-start | bytes 589828
  11.0 192.1 %copy-start.26 = (bf16[128,768]{1,0:T(8,128)(2,1)}, bf16[128,768]{1,0:T(8,128)(2,1)S(1)}, u32[]{:S(2)}) copy-start(bf16[128,768]{1,0:T(8,128)(2,1)S(1)} %get-tuple-element.755) | copy-start | bytes 589828
  85.5 27.5 %copy-start.19 = (bf16[1,128,768]{2,1,0:T(8,128)(2,1)S(1)}, bf16[1,128,768]{2,1,0:T(8,128)(2,1)}, u32[]{:S(2)}) copy-start(bf16[1,128,768]{2,1,0:T(8,128)(2,1)} %param.31) | copy-start | bytes 589828
  86.6 116.5 %copy-start.68 = (f32[3072]{0:T(1024)S(1)}, f32[3072]{0:T(1024)}, u32[]{:S(2)}) copy-start(f32[3072]{0:T(1024)} %param.43) | copy-start | bytes 36868
  86.6 273.6 %all-gather.21.cloned.1.call-start = ((), (), s32[]{:S(2)}) async-start(), calls=%async_computation.5 | async-start | bytes 3538944 | tf_op jit(solution)/shard_map/all_gather | solution.py:286
  115.5 471.2 %all-gather.27.cloned.1.call-start = ((), (), s32[]{:S(2)}) async-start(), calls=%async_computation.8 | async-start | bytes 3932160 | tf_op jit(solution)/shard_map/all_gather | solution.py:370
  210.9 379.6 %all-gather.25.cloned.1.call-start = ((), (), s32[]{:S(2)}) async-start(), calls=%async_computation.7 | async-start | bytes 3932160 | tf_op jit(solution)/shard_map/all_gather | solution.py:367
  220.4 72.1 %copy-start.69 = (f32[128,3072]{1,0:T(8,128)S(1)}, f32[128,3072]{1,0:T(8,128)}, u32[]{:S(2)}) copy-start(f32[128,3072]{1,0:T(8,128)} %get-tuple-element.784) | copy-start | bytes 4718596
  300.6 293.8 %all-gather.23.cloned.1.call-start = ((), (), s32[]{:S(2)}) async-start(), calls=%async_computation.6 | async-start | bytes 2949120 | tf_op jit(solution)/shard_map/all_gather | solution.py:366
  383.7 3.4 copy-start.44
  383.7 3.4 copy-start.49
  384.9 2.1 copy-start.42
  387.1 18.4 %copy-start.33 = (s32[64]{0:T(128)S(1)}, s32[64]{0:T(128)}, u32[]{:S(2)}) copy-start(s32[64]{0:T(128)} %get-tuple-element.1593) | copy-start | bytes 772
  387.1 18.4 %copy-start.35 = (s32[64]{0:T(128)S(1)}, s32[64]{0:T(128)}, u32[]{:S(2)}) copy-start(s32[64]{0:T(128)} %get-tuple-element.1595) | copy-start | bytes 772
  387.3 2.0 copy-start.9
  388.4 3.0 copy-start.37
  388.4 3.0 copy-start.40
  397.1 3.0 copy-start.37
  397.1 3.0 copy-start.40
  405.5 8.6 %copy-start.43 = (f32[12,128]{1,0:T(8,128)S(1)}, f32[12,128]{1,0:T(8,128)}, u32[]{:S(2)}) copy-start(f32[12,128]{1,0:T(8,128)} %copy-done.42) | copy-start | bytes 18436
  436.1 4.7 copy-start.63
  436.1 6.9 %copy-start.38 = (s32[64]{0:T(128)S(1)}, s32[64]{0:T(128)}, u32[]{:S(2)}) copy-start(s32[64]{0:T(128)} %get-tuple-element.1598) | copy-start | bytes 772
  436.1 6.9 %copy-start.41 = (s32[64]{0:T(128)S(1)}, s32[64]{0:T(128)}, u32[]{:S(2)}) copy-start(s32[64]{0:T(128)} %get-tuple-element.1600) | copy-start | bytes 772
  456.0 19.5 %copy-start.46 = (f32[128,8]{0,1:T(8,128)S(1)}, f32[128,8]{0,1:T(8,128)}, u32[]{:S(2)}) copy-start(f32[128,8]{0,1:T(8,128)} %copy-done.45) | copy-start | bytes 12292
  456.0 19.6 %copy-start.48 = (f32[128,8]{0,1:T(8,128)S(1)}, f32[128,8]{0,1:T(8,128)}, u32[]{:S(2)}) copy-start(f32[128,8]{0,1:T(8,128)} %copy-done.47) | copy-start | bytes 12292
  475.5 2.4 copy-start.4
  475.5 2.4 copy-start.5
  478.1 2.3 copy-start.18
  479.4 23.1 %copy-start.20 = (bf16[1,128,768]{2,1,0:T(8,128)(2,1)S(1)}, bf16[1,128,768]{2,1,0:T(8,128)(2,1)}, u32[]{:S(2)}) copy-start(bf16[1,128,768]{2,1,0:T(8,128)(2,1)} %param.31) | copy-start | bytes 589828
  480.4 81.6 %copy-start.15 = (bf16[128,3072]{1,0:T(8,128)(2,1)S(1)}, bf16[128,3072]{1,0:T(8,128)(2,1)}, u32[]{:S(2)}) copy-start(bf16[128,3072]{1,0:T(8,128)(2,1)} %get-tuple-element.745) | copy-start | bytes 2359300
  480.4 191.9 %all-reduce.4.cloned.1.call-start = ((), (), s32[]{:S(2)}) async-start(), calls=%async_computation.9 | async-start | bytes 7077888 | tf_op jit(solution)/shard_map/psum | solution.py:375
  562.0 4.9 copy-start.3
  562.0 4.9 copy-start.50
  567.0 23.4 %copy-start.21 = (bf16[128,768]{0,1:T(8,128)(2,1)}, bf16[128,768]{0,1:T(8,128)(2,1)S(1)}, u32[]{:S(2)}) copy-start(bf16[128,768]{0,1:T(8,128)(2,1)S(1)} %fusion.107) | copy-start | bytes 589828
  599.4 4.6 copy-start.11
  599.4 4.6 copy-start.13
  599.4 4.6 copy-start.16
  599.4 4.6 copy-start.23
  599.4 4.6 copy-start.52
  599.4 4.6 copy-start.54
  599.4 4.6 copy-start.58
  599.4 4.6 copy-start.66
  605.5 41.9 %copy-start.12 = (bf16[768,768]{0,1:T(8,128)(2,1)S(1)}, bf16[768,768]{0,1:T(8,128)(2,1)}, u32[]{:S(2)}) copy-start(bf16[768,768]{0,1:T(8,128)(2,1)} %all-gather.15.cloned.1.call-done) | copy-start | bytes 3538948
  605.6 41.9 %copy-start.22 = (bf16[128,768]{0,1:T(8,128)(2,1)S(1)}, bf16[128,768]{0,1:T(8,128)(2,1)}, u32[]{:S(2)}) copy-start(bf16[128,768]{0,1:T(8,128)(2,1)} %copy-done.21) | copy-start | bytes 589828
  605.6 41.9 %copy-start.61 = (f32[768]{0:T(1024)S(1)}, f32[768]{0:T(1024)}, u32[]{:S(2)}) copy-start(f32[768]{0:T(1024)} %param.45) | copy-start | bytes 9220
  605.6 41.9 %copy-start.62 = (f32[768]{0:T(1024)S(1)}, f32[768]{0:T(1024)}, u32[]{:S(2)}) copy-start(f32[768]{0:T(1024)} %param.41) | copy-start | bytes 9220
  647.4 31.7 %copy-start.64 = (f32[768]{0:T(1024)}, f32[768]{0:T(1024)S(1)}, u32[]{:S(2)}) copy-start(f32[768]{0:T(1024)S(1)} %get-tuple-element.1532) | copy-start | bytes 9220
  672.3 3.0 copy-start.24
  (25 other events, 25.4 us)
Sparse Core Ops, SparseCore 0:
  9.6 72.6 all-gather.10
  83.9 29.0 all-gather.14
  114.5 88.5 all-gather.16
  204.5 87.8 all-gather.18
  294.7 30.7 all-gather.12
  327.9 32.3 all-gather.20
  361.8 63.4 all-gather.26
  427.4 65.6 all-gather.24
  495.3 75.0 all-gather.22
  598.4 73.8 all-reduce.3
where the time goes:
time: 691 us; the launch traced here: 687 us
  waiting for transfers between devices  337 us (49%)
  blocking collectives  161 us (23%)
  matrix products  81.5 us (12%)
  local copies, waits for them, and re-layouts  52.1 us (8%)
  other arithmetic  36.8 us (5%)
  between operations  17.1 us (2%)
    all_gather x1, waiting for transfers between devices, local(): lax.all_gather(up_weight, 'fsdp', axis=0, tiled=True)  87.5 us
    all_gather x1, waiting for transfers between devices, local(): lax.all_gather(joined_weight, 'fsdp', axis=0, tiled=True)  71.3 us
    all_gather x1, waiting for transfers between devices, local(): lax.all_gather(down_weight, 'fsdp', axis=1, tiled=True)  68.6 us
    psum x1, blocking collectives, local(): lax.psum((gain_attn, shift_attn, gain_mlp, shift_mlp, jnp.sum(d_joined, 0...  40.8 us
    all_gather x1, waiting for transfers between devices, local(): lax.all_gather(jnp.concatenate([queries, d_mix_flat], 1), 'ctx', axis=0,...  32 us
    all_gather x1, blocking collectives, local(): n_mlp = lax.all_gather(norm_mlp, 'fsdp', axis=0, tiled=True)  30.9 us
    all_gather x1, blocking collectives, local(): g_out = lax.all_gather(grad_out, 'fsdp', axis=0, tiled=True)  28.5 us
    all_gather x1, waiting for transfers between devices, local(): lax.all_gather(attn_weight, 'fsdp', axis=1, tiled=True)  26.3 us
  transfers between devices with their start and end apart: 10, of which 7 were waited for; matrix products, arithmetic and copies ran while one was open for 22% of the time, Pallas kernels for 0%

commit v1 on v0

--- a/solution.py
+++ b/solution.py
@@ -1,6 +1,8 @@
 import jax
 import jax.numpy as jnp
 from jax import lax
+from jax.experimental import pallas as pl
+from jax.experimental.pallas import tpu as pltpu
 from jax.sharding import PartitionSpec as P
 
 HEADS = 12
@@ -428,9 +430,488 @@
     )
 
 
+CHIPS = 4
+DEPTH = 4
+MESH = pl.DeviceIdType.MESH
+VMEM_SPEC = pl.BlockSpec(memory_space=pltpu.VMEM)
+ANY_SPEC = pl.BlockSpec(memory_space=pl.ANY)
+
+
+def push(source, target, send_sem, recv_sem, **where):
+    return pltpu.make_async_remote_copy(
+        src_ref=source,
+        dst_ref=target,
+        send_sem=send_sem,
+        recv_sem=recv_sem,
+        device_id=where,
+        device_id_type=MESH,
+    )
+
+
+def greet(count_ctx, me, other):
+    barrier = pltpu.get_barrier_semaphore()
+    for step in range(1, DEPTH):
+        pl.semaphore_signal(
+            barrier, inc=1, device_id={"fsdp": (other + step) % DEPTH}, device_id_type=MESH
+        )
+    for target in count_ctx:
+        pl.semaphore_signal(barrier, inc=1, device_id={"ctx": target}, device_id_type=MESH)
+    pl.semaphore_wait(barrier, DEPTH - 1 + len(count_ctx))
+
+
+def gather_kernel(a_ref, b_ref, a_all, b_all, own_sem, zs, zr, cs, cr, ss, sr):
+    me = lax.axis_index("ctx")
+    depth = lax.axis_index("fsdp")
+    core = me % 2
+    chip = me // 2
+    sibling = me + 1 - 2 * core
+    greet([((chip + k) % CHIPS) * 2 + core for k in range(1, CHIPS)] + [sibling], me, depth)
+    sends = []
+    for k in range(1, CHIPS):
+        target = ((chip + k) % CHIPS) * 2 + core
+        sends.append(push(a_ref, a_all.at[me], cs.at[k - 1], cr.at[k - 1], ctx=target))
+        sends.append(
+            push(
+                b_ref,
+                b_all.at[depth],
+                zs.at[k - 1],
+                zr.at[k - 1],
+                fsdp=(depth + k) % DEPTH,
+            )
+        )
+    sends.append(push(a_ref, a_all.at[me], ss.at[0], sr.at[0], ctx=sibling))
+    own = [
+        pltpu.make_async_copy(a_ref, a_all.at[me], own_sem.at[0]),
+        pltpu.make_async_copy(b_ref, b_all.at[depth], own_sem.at[1]),
+    ]
+    for copy in sends + own:
+        copy.start()
+    for k in range(1, CHIPS):
+        source = ((chip + CHIPS - k) % CHIPS) * 2 + core
+        block = a_all.at[source]
+        push(block, block, cs.at[k - 1], cr.at[k - 1], ctx=sibling).wait_recv()
+        onward = push(block, block, ss.at[k], sr.at[k], ctx=sibling)
+        onward.start()
+        sends.append(onward)
+    for k in range(CHIPS):
+        source = ((chip + CHIPS - k) % CHIPS) * 2 + 1 - core
+        block = a_all.at[source]
+        push(block, block, ss.at[k], sr.at[k], ctx=sibling).wait_recv()
+    for k in range(1, DEPTH):
+        block = b_all.at[(depth + DEPTH - k) % DEPTH]
+        push(block, block, zs.at[k - 1], zr.at[k - 1], fsdp=depth).wait_recv()
+    for copy in sends:
+        copy.wait_send()
+    for copy in own:
+        copy.wait()
+
+
+def gather_all(rows, weights):
+    dma = pltpu.SemaphoreType.DMA
+    return pl.pallas_call(
+        gather_kernel,
+        out_shape=(
+            jax.ShapeDtypeStruct((2 * CHIPS,) + rows.shape, rows.dtype),
+            jax.ShapeDtypeStruct((DEPTH,) + weights.shape, weights.dtype),
+        ),
+        in_specs=[ANY_SPEC] * 2,
+        out_specs=(ANY_SPEC, ANY_SPEC),
+        scratch_shapes=[dma((2,)), dma((3,)), dma((3,)), dma((3,)), dma((3,)), dma((4,)), dma((4,))],
+        compiler_params=pltpu.CompilerParams(collective_id=1, has_side_effects=True),
+    )(rows, weights)
+
+
+PIECES = 4
+
+
+def reduce_kernel(
+    y_ref, w_ref, s_ref, y_out, w_all, s_out,
+    pair, held, far, deep, small_z, small_c,
+    pair_s, pair_r, far_s, far_r, zs, zr, cs, cr, ss, sr, sz_s, sz_r, sc_s, sc_r,
+):
+    me = lax.axis_index("ctx")
+    depth = lax.axis_index("fsdp")
+    core = me % 2
+    chip = me // 2
+    sibling = me + 1 - 2 * core
+    context = 2 * CHIPS
+    greet([(me + k) % context for k in range(1, context)], me, depth)
+    part_rows = w_ref.shape[1] // PIECES
+    sends = []
+
+    def go(copy):
+        copy.start()
+        sends.append(copy)
+
+    def peer(k):
+        return ((chip + k) % CHIPS) * 2 + core
+
+    def origin(k):
+        return ((chip + CHIPS - k) % CHIPS) * 2 + core
+
+    for k in range(1, DEPTH):
+        target = (depth + k) % DEPTH
+        go(push(s_ref, small_z.at[depth], sz_s.at[k - 1], sz_r.at[k - 1], fsdp=target))
+    for k in (1, 2, 3, 0):
+        block = ((chip + k) % CHIPS) * 2 + 1 - core
+        go(push(y_ref.at[block], pair.at[k], pair_s.at[k], pair_r.at[k], ctx=sibling))
+    for piece in range(PIECES):
+        rows = pl.ds(piece * part_rows, part_rows)
+        for k in range(1, DEPTH):
+            target = (depth + k) % DEPTH
+            go(
+                push(
+                    w_ref.at[target, rows],
+                    deep.at[k - 1, rows],
+                    zs.at[piece, k - 1],
+                    zr.at[piece, k - 1],
+                    fsdp=target,
+                )
+            )
+    for k in (1, 2, 3, 0):
+        push(pair.at[k], pair.at[k], pair_s.at[k], pair_r.at[k], ctx=sibling).wait_recv()
+        joint = y_ref[peer(k)].astype(jnp.float32) + pair[k].astype(jnp.float32)
+        if k:
+            held[k - 1] = joint.astype(jnp.bfloat16)
+            go(push(held.at[k - 1], far.at[k - 1], far_s.at[k - 1], far_r.at[k - 1], ctx=peer(k)))
+        else:
+            y_out[...] = joint
+    small_z[depth] = s_ref[...]
+    for k in range(1, DEPTH):
+        slot = small_z.at[(depth + DEPTH - k) % DEPTH]
+        push(slot, slot, sz_s.at[k - 1], sz_r.at[k - 1], fsdp=depth).wait_recv()
+    small_c[me] = (small_z[0] + small_z[1]) + (small_z[2] + small_z[3])
+    for k in range(1, context):
+        slot = small_c.at[me]
+        go(push(slot, slot, sc_s.at[k - 1], sc_r.at[k - 1], ctx=(me + k) % context))
+
+    def hand_on(piece):
+        rows = pl.ds(piece * part_rows, part_rows)
+        for k in range(1, CHIPS):
+            block = w_all.at[origin(k), rows]
+            push(block, block, cs.at[piece, k - 1], cr.at[piece, k - 1], ctx=sibling).wait_recv()
+            go(push(block, block, ss.at[piece, k], sr.at[piece, k], ctx=sibling))
+
+    for piece in range(PIECES):
+        rows = pl.ds(piece * part_rows, part_rows)
+        total = w_ref[depth, rows].astype(jnp.float32)
+        for k in range(1, DEPTH):
+            slot = deep.at[k - 1, rows]
+            push(slot, slot, zs.at[piece, k - 1], zr.at[piece, k - 1], fsdp=depth).wait_recv()
+            total = total + deep[k - 1, rows].astype(jnp.float32)
+        w_all[me, rows] = total.astype(jnp.bfloat16)
+        block = w_all.at[me, rows]
+        for k in range(1, CHIPS):
+            go(push(block, block, cs.at[piece, k - 1], cr.at[piece, k - 1], ctx=peer(k)))
+        go(push(block, block, ss.at[piece, 0], sr.at[piece, 0], ctx=sibling))
+        if piece:
+            hand_on(piece - 1)
+    for k in range(1, CHIPS):
+        slot = far.at[k - 1]
+        push(slot, slot, far_s.at[k - 1], far_r.at[k - 1], ctx=sibling).wait_recv()
+        y_out[...] += far[k - 1].astype(jnp.float32)
+    for k in range(1, context):
+        slot = small_c.at[(me + context - k) % context]
+        push(slot, slot, sc_s.at[k - 1], sc_r.at[k - 1], ctx=sibling).wait_recv()
+    total = small_c[0]
+    for k in range(1, context):
+        total = total + small_c[k]
+    s_out[...] = total
+    hand_on(PIECES - 1)
+    for piece in range(PIECES):
+        rows = pl.ds(piece * part_rows, part_rows)
+        for k in range(CHIPS):
+            block = w_all.at[((chip + CHIPS - k) % CHIPS) * 2 + 1 - core, rows]
+            push(block, block, ss.at[piece, k], sr.at[piece, k], ctx=sibling).wait_recv()
+    for copy in sends:
+        copy.wait_send()
+
+
+def reduce_all(partial, weight_grads, small):
+    context, rows, columns = partial.shape
+    dma = pltpu.SemaphoreType.DMA
+    return pl.pallas_call(
+        reduce_kernel,
+        out_shape=(
+            jax.ShapeDtypeStruct((rows, columns), jnp.float32),
+            jax.ShapeDtypeStruct((context,) + weight_grads.shape[1:], jnp.bfloat16),
+            jax.ShapeDtypeStruct(small.shape, jnp.float32),
+        ),
+        in_specs=[VMEM_SPEC] * 3,
+        out_specs=(VMEM_SPEC,) * 3,
+        scratch_shapes=[
+            pltpu.VMEM((CHIPS, rows, columns), jnp.bfloat16),
+            pltpu.VMEM((CHIPS - 1, rows, columns), jnp.bfloat16),
+            pltpu.VMEM((CHIPS - 1, rows, columns), jnp.bfloat16),
+            pltpu.VMEM((DEPTH - 1,) + weight_grads.shape[1:], jnp.bfloat16),
+            pltpu.VMEM((DEPTH,) + small.shape, jnp.float32),
+            pltpu.VMEM((context,) + small.shape, jnp.float32),
+        ]
+        + [dma((4,)), dma((4,)), dma((3,)), dma((3,))]
+        + [dma((PIECES, 3))] * 4
+        + [dma((PIECES, 4))] * 2
+        + [dma((3,)), dma((3,)), dma((7,)), dma((7,))],
+        compiler_params=pltpu.CompilerParams(
+            collective_id=2, has_side_effects=True, vmem_limit_bytes=40 * 1024 * 1024
+        ),
+    )(partial, weight_grads, small)
+
+
+Q_TILE = 256
+PAIR = 2 * HEAD
+
+
+def attention_kernel(
+    joined_ref, dmix_ref, cos_ref, down_ref, up_ref, q_pl, q_low, k_pl,
+    mix_ref, grad_ref, bias_ref, q_s, k_s, v_s, g_s, dk_s, dv_s,
+):
+    length = joined_ref.shape[0]
+    scale = HEAD ** (-0.5)
+    half = ROT // 2
+    dot = lambda a, b, dims: lax.dot_general(a, b, dims, preferred_element_type=jnp.float32)
+    contract_inner = (((1,), (0,)), ((), ()))
+
+    def turn(block, sign):
+        return (
+            block * cos_ref[...]
+            + pltpu.roll(block, PAIR - half, 1) * (sign * down_ref[...])
+            + pltpu.roll(block, half, 1) * (sign * up_ref[...])
+        )
+
+    query = turn(joined_ref[:, :PAIR], 1.0)
+    key = turn(joined_ref[:, PAIR : 2 * PAIR], 1.0)
+    value = joined_ref[:, 2 * PAIR :]
+    mix_grad = dmix_ref[...].astype(jnp.float32)
+    lane = lax.broadcasted_iota(jnp.int32, (1, PAIR), 1)
+    for head in range(2):
+        own = (lane // HEAD) == head
+        q_s[head] = jnp.where(own, query, 0.0).astype(jnp.bfloat16)
+        k_s[head] = jnp.where(own, key, 0.0).astype(jnp.bfloat16)
+        v_s[head] = jnp.where(own, value, 0.0).astype(jnp.bfloat16)
+        g_s[head] = jnp.where(own, mix_grad, 0.0).astype(jnp.bfloat16)
+    dk_s[...] = jnp.zeros_like(dk_s)
+    dv_s[...] = jnp.zeros_like(dv_s)
+    key_place = k_pl[...]
+    dq_parts = []
+    for tile in range(length // Q_TILE):
+        rows = slice(tile * Q_TILE, (tile + 1) * Q_TILE)
+        valid = (key_place <= q_pl[rows, :]) & (key_place >= q_low[rows, :])
+        mixed = jnp.zeros((Q_TILE, PAIR), jnp.float32)
+        d_query = jnp.zeros((Q_TILE, PAIR), jnp.float32)
+        for head in range(2):
+            q_t = q_s[head, rows, :]
+            g_t = g_s[head, rows, :]
+            score = jnp.where(valid, dot(q_t, k_s[head], contract_cols) * scale, masked_score)
+            top = jnp.max(score, -1, keepdims=True)
+            weight = jnp.exp(score - top)
+            prob = weight * (1.0 / jnp.sum(weight, -1, keepdims=True))
+            prob_low = prob.astype(jnp.bfloat16)
+            mix_h = dot(prob_low, v_s[head], contract_inner)
+            delta = jnp.sum(g_t.astype(jnp.float32) * mix_h, -1, keepdims=True)
+            d_prob = dot(g_t, v_s[head], contract_cols)
+            d_score = (prob * (d_prob - delta)).astype(jnp.bfloat16)
+            d_query += dot(d_score, k_s[head], contract_inner)
+            dk_s[...] += dot(d_score, q_t, contract_rows)
+            dv_s[...] += dot(prob_low, g_t, contract_rows)
+            mixed += mix_h
+        mix_ref[rows, :] = mixed.astype(jnp.bfloat16)
+        dq_parts.append(d_query)
+    d_q = turn(jnp.concatenate(dq_parts, 0) * scale, -1.0)
+    d_k = turn(dk_s[...] * scale, -1.0)
+    for index, block in enumerate((d_q, d_k, dv_s[...])):
+        columns = slice(index * PAIR, (index + 1) * PAIR)
+        grad_ref[:, columns] = block.astype(jnp.bfloat16)
+        bias_ref[:, columns] = jnp.sum(block, 0, keepdims=True)
+
+
+def attention(joined, d_mix, tables, places, lowest):
+    length = joined.shape[0]
+    keep = [pltpu.VMEM((2, length, PAIR), jnp.bfloat16)] * 4
+    return pl.pallas_call(
+        attention_kernel,
+        out_shape=(
+            jax.ShapeDtypeStruct((length, PAIR), jnp.bfloat16),
+            jax.ShapeDtypeStruct((length, 3 * PAIR), jnp.bfloat16),
+            jax.ShapeDtypeStruct((1, 3 * PAIR), jnp.float32),
+        ),
+        in_specs=[VMEM_SPEC] * 8,
+        out_specs=(VMEM_SPEC,) * 3,
+        scratch_shapes=keep + [pltpu.VMEM((length, PAIR), jnp.float32)] * 2,
+        compiler_params=pltpu.CompilerParams(vmem_limit_bytes=48 * 1024 * 1024),
+    )(joined, d_mix, *tables, places[:, None], lowest[:, None], places[None, :])
+
+
+def split_local(
+    layer_input,
+    cotangent,
+    block_order,
+    boundary,
+    attn_gain,
+    attn_shift,
+    mlp_gain,
+    mlp_shift,
+    joined_weight,
+    joined_bias,
+    attn_weight,
+    attn_bias,
+    up_weight,
+    up_bias,
+    down_weight,
+    down_bias,
+):
+    rows = layer_input.shape[1]
+    width = layer_input.shape[2]
+    context = 2 * CHIPS
+    length = rows * context
+    half = rows // 2
+    holders = HEADS // 2
+    shard = joined_weight.shape[0]
+    units = up_weight.shape[1] // context
+    me = lax.axis_index("ctx")
+    slot = jnp.minimum(me, holders - 1)
+    holds = me < holders
+
+    own_joined = lax.dynamic_slice(
+        joined_weight.reshape(shard, 3, width), (0, 0, slot * PAIR), (shard, 3, PAIR)
+    ).reshape(shard, 3 * PAIR)
+    own_attn = lax.dynamic_slice(attn_weight, (slot * PAIR, 0), (PAIR, shard)).T
+    own_up = lax.dynamic_slice(up_weight, (0, me * units), (shard, units))
+    own_down = lax.dynamic_slice(down_weight, (me * units, 0), (units, shard)).T
+    own_weights = jnp.concatenate(
+        [
+            jnp.where(holds, own_joined, 0),
+            own_up,
+            own_down,
+            jnp.where(holds, own_attn, 0),
+        ],
+        1,
+    )
+    own_rows = jnp.concatenate([layer_input[0], cotangent[0]], 1)
+    rows_all, weights_all = gather_all(own_rows, own_weights)
+    rows_all = rows_all.reshape(length, 2 * width)
+    weights_all = weights_all.reshape(width, -1)
+    w_joined = weights_all[:, : 3 * PAIR]
+    w_up = weights_all[:, 3 * PAIR : 3 * PAIR + units]
+    w_out = weights_all[:, 3 * PAIR + units :]
+    hidden = rows_all[:, :width].astype(jnp.float32)
+    grad_out = rows_all[:, width:]
+    b_joined = jnp.where(
+        holds,
+        lax.dynamic_slice(joined_bias.reshape(3, width), (0, slot * PAIR), (3, PAIR)),
+        0.0,
+    ).reshape(3 * PAIR)
+    b_up = lax.dynamic_slice(up_bias, (me * units,), (units,))
+
+    places = place_lookup(block_order, jnp.int32(0), length, half)
+    lowest = jnp.where(places >= boundary[0], boundary[0], 0)
+    lane = jnp.arange(PAIR, dtype=jnp.int32) % HEAD
+    bend = ROT // 2
+    freq = 10000.0 ** (-2.0 * (lane % bend).astype(jnp.float32) / ROT)
+    angles = places.astype(jnp.float32)[:, None] * freq[None, :]
+    cosine = jnp.where(lane < ROT, jnp.cos(angles), 1.0)
+    sine = jnp.sin(angles)
+    tables = (
+        cosine,
+        jnp.where(lane < bend, -sine, 0.0),
+        jnp.where((lane >= bend) & (lane < ROT), sine, 0.0),
+    )
+
+    normal, _ = normalize_parts(hidden)
+    norm_attn = (normal * attn_gain + attn_shift).astype(jnp.bfloat16)
+    norm_mlp = (normal * mlp_gain + mlp_shift).astype(jnp.bfloat16)
+    joined = jnp.dot(norm_attn, w_joined, preferred_element_type=jnp.float32) + b_joined
+    upper = jnp.dot(norm_mlp, w_up, preferred_element_type=jnp.float32) + b_up
+    d_out = jnp.dot(grad_out, w_out, preferred_element_type=jnp.float32)
+    d_act = d_out[:, :units]
+    d_mix = d_out[:, units:].astype(jnp.bfloat16)
+    mix_low, d_joined_low, joined_sums = attention(joined, d_mix, tables, places, lowest)
+    act, gelu_pull = jax.vjp(lambda argument: jax.nn.gelu(argument, approximate=False), upper)
+    d_up = gelu_pull(d_act)[0]
+    d_up_low = d_up.astype(jnp.bfloat16)
+    outer = jnp.concatenate([act.astype(jnp.bfloat16), mix_low], 1)
+    branches = lax.dot_general(outer, w_out, contract_cols, preferred_element_type=jnp.float32)
+    d_norm_attn = lax.dot_general(
+        d_joined_low, w_joined, contract_cols, preferred_element_type=jnp.float32
+    )
+    d_norm_mlp = lax.dot_general(d_up_low, w_up, contract_cols, preferred_element_type=jnp.float32)
+    scaled = d_norm_attn * attn_gain + d_norm_mlp * mlp_gain
+    partial = jnp.concatenate([branches, scaled], 1).astype(jnp.bfloat16)
+    weight_grads = jnp.concatenate(
+        [
+            lax.dot_general(norm_attn, d_joined_low, contract_rows, preferred_element_type=jnp.float32),
+            lax.dot_general(norm_mlp, d_up_low, contract_rows, preferred_element_type=jnp.float32),
+            lax.dot_general(grad_out, outer, contract_rows, preferred_element_type=jnp.float32),
+        ],
+        1,
+    ).astype(jnp.bfloat16)
+    mine = jnp.arange(context, dtype=jnp.int32) == me
+    spread_joined = jnp.where(
+        mine[:holders][None, :, None], joined_sums.reshape(3, 1, PAIR), 0.0
+    ).reshape(-1)
+    spread_up = jnp.where(mine[:, None], jnp.sum(d_up, 0)[None, :], 0.0).reshape(-1)
+    small = jnp.concatenate(
+        [
+            jnp.sum(d_norm_attn * normal, 0),
+            jnp.sum(d_norm_attn, 0),
+            jnp.sum(d_norm_mlp * normal, 0),
+            jnp.sum(d_norm_mlp, 0),
+            spread_joined,
+            jnp.sum(cotangent[0].astype(jnp.float32), 0),
+            spread_up,
+        ]
+    )
+    sums, grads, small = reduce_all(
+        partial.reshape(context, rows, 2 * width),
+        weight_grads.reshape(DEPTH, shard, -1),
+        small.reshape(-1, 128),
+    )
+    small = small.reshape(-1)
+    own_hidden = layer_input[0].astype(jnp.float32)
+    layer_output = (own_hidden + sums[:, :width] + attn_bias + down_bias).astype(jnp.bfloat16)
+    own_normal, own_inverse = normalize_parts(own_hidden)
+    inner = sums[:, width:]
+    back = own_inverse * (
+        inner
+        - jnp.mean(inner, -1, keepdims=True)
+        - own_normal * jnp.mean(inner * own_normal, -1, keepdims=True)
+    )
+    input_grad = cotangent[0].astype(jnp.float32) + back
+    ends = (3 * PAIR, 3 * PAIR + units, 3 * PAIR + 2 * units)
+    dfused = (
+        grads[:holders, :, : ends[0]]
+        .reshape(holders, shard, 3, PAIR)
+        .transpose(1, 2, 0, 3)
+        .reshape(shard, 3 * width)
+        .astype(jnp.float32)
+    )
+    dup = grads[:, :, ends[0] : ends[1]].transpose(1, 0, 2).reshape(shard, -1).astype(jnp.float32)
+    ddown = grads[:, :, ends[1] : ends[2]].transpose(0, 2, 1).reshape(-1, shard).astype(jnp.float32)
+    dattn = grads[:holders, :, ends[2] :].transpose(0, 2, 1).reshape(width, shard)
+    base = 4 * width
+    fused_end = base + 3 * width
+    out_end = fused_end + width
+    return (
+        layer_output[None],
+        input_grad[None],
+        small[:width],
+        small[width : 2 * width],
+        small[2 * width : 3 * width],
+        small[3 * width : base],
+        dfused,
+        small[base:fused_end],
+        dattn.astype(jnp.float32),
+        small[fused_end:out_end],
+        dup,
+        small[out_end:],
+        ddown,
+        small[fused_end:out_end],
+    )
+
+
 def solution(mesh):
+    split = mesh.shape["ctx"] == 2 * CHIPS and mesh.shape["fsdp"] == DEPTH
     return jax.shard_map(
-        local,
+        split_local if split else local,
         mesh=mesh,
         in_specs=(
             P("fsdp", "ctx", None),

time: 691 us -> 189 us (0.27)
  waiting for transfers between devices: 337 us -> 0 us
  blocking collectives: 161 us -> 0 us
  Pallas kernels: 0 us -> 116 us
  matrix products: 81.5 us -> 23.4 us
  local copies, waits for them, and re-layouts: 52.1 us -> 24.7 us
  between operations: 17.1 us -> 1.93 us
  other arithmetic: 36.8 us -> 22 us
    all_gather x9 -> x0, waiting for transfers between devices: 311 us -> none  [the longest x1 87.5 us: local(): lax.all_gather(up_weight, 'fsdp', axis=0, tiled=True)]
    all_gather x5 -> x0, blocking collectives: 120 us -> none  [the longest x1 30.9 us: local(): n_mlp = lax.all_gather(norm_mlp, 'fsdp', axis=0, tiled=True)]
    pallas_call x0 -> x3, Pallas kernels: none -> 116 us  [the longest x1 63.7 us: reduce_all(): pl.pallas_call(reduce_kernel, out_shape=(jax.ShapeDtypeStruct((rows, colu...]
    dot_general x33 -> x9, matrix products: 81.5 us -> 23.4 us  [the longest x1 7.12 us: split_local(): upper = jnp.dot(norm_mlp, w_up, preferred_element_type=jnp.float32) + b_up]
    psum x1 -> x0, blocking collectives: 40.8 us -> none  [local(): lax.psum((gain_attn, shift_attn, gain_mlp, shift_mlp, jnp.sum(d_joined, 0...]
    psum x1 -> x0, waiting for transfers between devices: 23.6 us -> none  [local(): lax.psum(lax.dot_general(cols_attn, g_joined, contract_rows, preferred_el...]
    while x63 -> x0, local copies, waits for them, and re-layouts: 16.9 us -> none  [the longest x5 7.73 us: local(): lax.fori_loop(first_tile, jnp.int32(tiles_all), owner_step, (zero_heads,...]
    convert_element_type x19 -> x3, other arithmetic: 14 us -> 2.42 us  [the longest x1 1.33 us: split_local(): dfused = grads[:holders, :, :ends[0]].reshape(holders, shard, 3, PAIR).tr...]
  transfers between devices with their start and end apart: 10 -> 0, of which waited for: 7 -> 0; matrix products, arithmetic and copies ran while one was open for 22% -> 0% of each run, Pallas kernels for 0% -> 0%
where the time goes in v1:
time: 189 us; the launch traced here: 188 us
  Pallas kernels  116 us (61%)
  local copies, waits for them, and re-layouts  24.7 us (13%)
  matrix products  23.4 us (12%)
  other arithmetic  22 us (12%)
  between operations  1.93 us (1%)
    pallas_call x1, Pallas kernels, reduce_all(): pl.pallas_call(reduce_kernel, out_shape=(jax.ShapeDtypeStruct((rows, colu...  63.7 us
    pallas_call x1, Pallas kernels, gather_all(): pl.pallas_call(gather_kernel, out_shape=(jax.ShapeDtypeStruct((2 * CHIPS,...  40.2 us
    pallas_call x1, Pallas kernels, attention(): pl.pallas_call(attention_kernel, out_shape=(jax.ShapeDtypeStruct((length,...  11.6 us
    convert_element_type x3, local copies, waits for them, and re-layouts, split_local(): dfused = grads[:holders, :, :ends[0]].reshape(holders, shard, 3, PAIR).tr...  7.87 us
    dot_general x1, matrix products, split_local(): upper = jnp.dot(norm_mlp, w_up, preferred_element_type=jnp.float32) + b_up  7.12 us
    unnamed x58, local copies, waits for them, and re-layouts  5.75 us
    dot_general x1, matrix products, split_local(): lax.dot_general(norm_attn, d_joined_low, contract_rows, preferred_element...  3.85 us

profile of v1, /device:TPU:0, one launch (start us, length us, event | category | flops | bytes accessed | tf_op | source)
XLA Modules:
  0.0 187.5 jit_solution(14215532475191420030)
XLA Ops:
  0.6 0.0 copy-start
  1.4 1.0 convert_reduce_fusion.1
  2.5 1.1 fusion.45
  3.7 0.8 dynamic_slice.22
  4.4 1.0 convert_reduce_fusion.2
  5.4 0.7 select_reduce_fusion
  6.2 0.7 reshape.264
  6.9 0.8 select_bitcast_fusion
  7.8 0.9 dynamic-slice_bitcast_fusion
  8.7 1.8 pad_maximum_fusion.6.a_ref
  10.5 0.2 copy.36
  10.7 0.1 compare_select_fusion
  10.8 3.1 %reshape.261 = bf16[192,3,768]{2,1,0:T(4,128)(2,1)} reshape(bf16[192,2304]{1,0:T(8,128)(2,1)} %param.24) | data formatting | bytes 1769472 | tf_op jit(solution)/shard_map/reshape | solution.py:775
  13.9 1.0 dynamic-slice_select_fusion
  15.0 0.8 pad_maximum_fusion.5.b_ref
  15.8 3.0 %fusion.22 = (f32[1024,128]{1,0:T(8,128)S(1)}, f32[1024,128]{1,0:T(8,128)S(1)}, f32[1024,128]{1,0:T(8,128)}) fusion(f32[128]{0:T(128)S(1)} %fusion.65, f32[1024]{0:T(1024)S(1)} %get-tuple-element.55, pred[128]{0:T(512)(128)(4,1)S(1)} %get-tuple-element.57, pred[128]{0:T(512)(128)(4,1)S(1)} %get-tuple-element.58, pred[128]{0:T(512)(128)(4,1)S(1)} %broadcast_compare_fusion.1), kind=kLoop, calls=%fused_computation.51 | loop fusion | flops 655360 | bytes 1577856 | tf_op jit(solution)/shard_map/jit(_where)/select_n | solution.py:816
  18.8 40.2 %shard_map.263 = (bf16[8,128,1536]{2,1,0:T(8,128)(2,1)}, bf16[4,192,1280]{2,1,0:T(8,128)(2,1)}) custom-call(bf16[128,1536]{1,0:T(8,128)(2,1)} %pad_maximum_fusion.6.a_ref, bf16[192,1280]{1,0:T(8,128)(2,1)} %pad_maximum_fusion.5.b_ref), custom_call_target="tpu_custom_call" | custom-call | tf_op jit(solution)/shard_map/pallas_call | solution.py:511
  59.0 0.0 copy-start.20
  59.0 0.0 copy-start.22
  59.0 1.8 convert_reduce_fusion
  60.9 2.0 %fusion.12 = f32[1024]{0:T(1024)S(1)} fusion(f32[1024]{0:T(1024)S(1)} %broadcast_multiply_fusion.1, bf16[1024,1536]{1,0:T(8,128)(2,1)} %bitcast.74), kind=kLoop, calls=%fused_computation.14 | loop fusion | flops 3144704 | bytes 1581056 | tf_op jit(solution)/shard_map/reduce_sum | solution.py:30
  62.9 2.2 %convolution_add_fusion.joined_ref = f32[1024,384]{1,0:T(8,128)S(1)} fusion(f32[384]{0:T(512)S(1)} %select_bitcast_fusion.1, bf16[768,1280]{1,0:T(8,128)(2,1)} %bitcast.92, f32[768]{0:T(1024)S(1)} %copy-done.20, f32[768]{0:T(1024)S(1)} %copy-done.22, f32[1024]{0:T(1024)S(1)} %add_rsqrt_fusion, f32[1024]{0:T(1024)S(1)} %broadcast_multiply_fusion.1, ...), kind=kOutput, calls=%fused_computation.38 | convolution fusion | flops 609091584 | bytes 3753984 | tf_op jit(solution)/shard_map/dot_general | solution.py:822
  65.1 2.2 %fusion.20 = f32[1024,512]{1,0:T(8,128)S(1)} fusion(bf16[1024,1536]{1,0:T(8,128)(2,1)S(1)} %bitcast.78, bf16[768,1280]{1,0:T(8,128)(2,1)} %bitcast.93), kind=kOutput, calls=%fused_computation.42 | convolution fusion | flops 805306368 | bytes 4456448 | tf_op jit(solution)/shard_map/dot_general | solution.py:824
  67.3 0.1 slice.166.dmix_ref
  67.4 11.6 %shard_map.264 = (bf16[1024,128]{1,0:T(8,128)(2,1)S(1)}, bf16[1024,384]{1,0:T(8,128)(2,1)S(1)}, f32[1,384]{1,0:T(1,128)S(1)}) custom-call(f32[1024,384]{1,0:T(8,128)S(1)} %convolution_add_fusion.joined_ref, bf16[1024,128]{1,0:T(8,128)(2,1)S(1)} %slice.166.dmix_ref, f32[1024,128]{1,0:T(8,128)S(1)} %copy-done.2, f32[1024,128]{1,0:T(8,128)S(1)} %get-tuple-element.52.down_ref, ...), custom_call_target="tpu_custom_call" | custom-call | tf_op jit(solution)/shard_map/pallas_call | solution.py:730
  79.0 0.0 copy-start.3
  79.0 0.9 copy-done.3
  79.9 0.7 copy-done.5
  80.6 0.1 broadcast_select_fusion.1
  80.7 0.0 copy-start.23
  80.7 3.9 %convolution_convert_fusion.3 = bf16[768,384]{1,0:T(8,128)(2,1)} fusion(bf16[1024,384]{1,0:T(8,128)(2,1)} %copy-done.3, f32[768]{0:T(1024)S(1)} %copy-done.20, f32[768]{0:T(1024)S(1)} %copy-done.22, f32[1024]{0:T(1024)S(1)} %add_rsqrt_fusion, f32[1024]{0:T(1024)S(1)} %broadcast_multiply_fusion.1, bf16[1024,1536]{1,0:T(8,128)(2,1)} %bitcast.75), kind=kOutput, calls=%fused_computation.45 | convolution fusion | flops 608993280 | bytes 2963456 | tf_op jit(solution)/shard_map/dot_general | solution.py:841
  84.6 7.1 %fusion.73 = (f32[384]{0:T(512)S(1)}, bf16[1024,384]{1,0:T(8,128)(2,1)}, f32[1024,384]{1,0:T(8,128)S(1)}, f32[1024,384]{1,0:T(8,128)}) fusion(f32[1024,512]{1,0:T(8,128)S(1)} %copy-done.16, f32[384]{0:T(512)S(1)} %dynamic_slice.22, bf16[768,1280]{1,0:T(8,128)(2,1)} %bitcast.94, f32[768]{0:T(1024)S(1)} %copy-done.21, f32[768]{0:T(1024)S(1)} %copy-done.23, ...), kind=kOutput, calls=%fused_computation.155 | convolution fusion | flops 637795968 | bytes 7687680 | tf_op jit(solution)/shard_map/dot_general | solution.py:823
  91.7 0.1 broadcast_select_fusion
  91.8 3.0 %convolution_convert_fusion.2 = bf16[768,384]{1,0:T(8,128)(2,1)S(1)} fusion(bf16[1024,384]{1,0:T(8,128)(2,1)} %get-tuple-element.37, f32[768]{0:T(1024)S(1)} %copy-done.21, f32[768]{0:T(1024)S(1)} %copy-done.23, f32[1024]{0:T(1024)S(1)} %add_rsqrt_fusion, f32[1024]{0:T(1024)S(1)} %broadcast_multiply_fusion.1, bf16[1024,1536]{1,0:T(8,128)(2,1)} %bitcast.76), kind=kOutput, calls=%fused_computation.44 | convolution fusion | flops 608993280 | bytes 2963456 | tf_op jit(solution)/shard_map/dot_general | solution.py:842
  94.8 0.2 multiply_convert_fusion
  95.1 0.7 copy-done.6
  95.8 1.0 copy-done.10
  96.8 1.0 convolution_convert_fusion.1
  97.8 0.1 copy-done.13
  97.9 0.1 pad_maximum_fusion.1.w_ref
  98.0 1.4 copy-done.14
  99.4 1.0 convolution_convert_fusion
  100.4 0.1 copy-done.4
  100.6 1.0 fusion.32
  101.6 0.1 copy-done.24
  101.7 2.1 %fusion.11 = (f32[768]{0:T(1024)S(1)}, f32[768]{0:T(1024)S(1)}, f32[768]{0:T(1024)S(1)}, f32[768]{0:T(1024)S(1)}, bf16[1024,768]{1,0:T(8,128)(2,1)S(1)}) fusion(f32[1024]{0:T(1024)S(1)} %add_rsqrt_fusion, f32[1024]{0:T(1024)S(1)} %broadcast_multiply_fusion.1, bf16[1024,1536]{1,0:T(8,128)(2,1)S(1)} %bitcast.81, f32[1024,768]{1,0:T(8,128)S(1)} %fusion.32, ...), kind=kOutput, calls=%fused_computation.13 | convolution fusion | flops 614200320 | bytes 7696384 | tf_op jit(solution)/shard_map/dot_general | solution.py:836
  103.9 0.3 pad_maximum_fusion.y_ref
  104.2 0.0 copy-start.18
  104.2 0.0 copy-start.19
  104.2 63.7 %shard_map.265 = (f32[128,1536]{1,0:T(8,128)S(1)}, bf16[8,192,1280]{2,1,0:T(8,128)(2,1)S(1)}, f32[72,128]{1,0:T(8,128)S(1)}) custom-call(bf16[8,128,1536]{2,1,0:T(8,128)(2,1)S(1)} %pad_maximum_fusion.y_ref, bf16[4,192,1280]{2,1,0:T(8,128)(2,1)S(1)} %pad_maximum_fusion.1.w_ref, f32[72,128]{1,0:T(8,128)S(1)} %bitcast.70), custom_call_target="tpu_custom_call" | custom-call | tf_op jit(solution)/shard_map/pallas_call | solution.py:633
  168.0 0.2 slice_reduce_fusion
  168.2 1.3 fusion.46
  169.5 0.6 slice_bitcast_fusion.1
  170.1 0.6 slice_bitcast_fusion
  170.7 0.6 slice_bitcast_fusion.2
  171.4 0.9 copy_bitcast_fusion
  172.2 1.3 slice_convert_fusion
  173.5 2.7 %reshape.270 = f32[6,192,3,128]{3,2,1,0:T(4,128)S(1)} reshape(f32[6,192,384]{2,1,0:T(8,128)} %slice_convert_fusion) | data formatting | bytes 3538944 | tf_op jit(solution)/shard_map/convert_element_type | solution.py:885
  176.2 2.5 %copy.37 = f32[192,3,6,128]{3,2,1,0:T(8,128)} copy(f32[192,3,6,128]{3,1,0,2:T(4,128)S(1)} %bitcast.71) | data formatting | bytes 3538944 | tf_op jit(solution)/shard_map/convert_element_type | solution.py:885
  178.7 2.7 %reshape.266 = f32[192,2304]{1,0:T(8,128)} reshape(f32[192,3,6,128]{3,2,1,0:T(8,128)} %copy.37) | data formatting | bytes 3538944 | tf_op jit(solution)/shard_map/convert_element_type | solution.py:885
  181.4 2.1 %convert_bitcast_fusion = (f32[8,24,8,384]{3,2,1,0:T(8,128)S(1)}, f32[8,24,8,384]{3,2,1,0:T(8,128)S(1)}) fusion(bf16[8,192,1280]{2,1,0:T(8,128)(2,1)} %copy-done.1), kind=kLoop, calls=%fused_computation.18 | loop fusion | flops 1179648 | bytes 7077888
  183.6 1.7 copy.43
  185.2 1.7 copy.42
  186.9 0.6 copy.57
  (62 shorter events, 0.3 us)
Async XLA Ops:
  0.6 7.1 %copy-start = (bf16[192,3072]{1,0:T(8,128)(2,1)S(1)}, bf16[192,3072]{1,0:T(8,128)(2,1)}, u32[]{:S(2)}) copy-start(bf16[192,3072]{1,0:T(8,128)(2,1)} %param.28) | copy-start | bytes 3538948
  59.0 3.9 %copy-start.8 = (bf16[8,128,1536]{2,1,0:T(8,128)(2,1)S(1)}, bf16[8,128,1536]{2,1,0:T(8,128)(2,1)}, u32[]{:S(2)}) copy-start(bf16[8,128,1536]{2,1,0:T(8,128)(2,1)} %get-tuple-element.22) | copy-start | bytes 9437188
  59.0 3.9 %copy-start.20 = (f32[768]{0:T(1024)S(1)}, f32[768]{0:T(1024)}, u32[]{:S(2)}) copy-start(f32[768]{0:T(1024)} %param.21) | copy-start | bytes 9220
  59.0 3.9 %copy-start.22 = (f32[768]{0:T(1024)S(1)}, f32[768]{0:T(1024)}, u32[]{:S(2)}) copy-start(f32[768]{0:T(1024)} %param.20) | copy-start | bytes 9220
  65.1 2.3 %copy-start.2 = (f32[1024,128]{1,0:T(8,128)S(1)}, f32[1024,128]{1,0:T(8,128)}, u32[]{:S(2)}) copy-start(f32[1024,128]{1,0:T(8,128)} %get-tuple-element.53.cos_ref) | copy-start | bytes 1572868
  67.3 11.7 %copy-start.15 = (f32[1024,512]{1,0:T(8,128)}, f32[1024,512]{1,0:T(8,128)S(1)}, u32[]{:S(2)}) copy-start(f32[1024,512]{1,0:T(8,128)S(1)} %fusion.20) | copy-start | bytes 6291460
  79.0 0.9 copy-start.3
  79.9 0.7 copy-start.5
  80.7 3.9 %copy-start.9 = (bf16[8,128,1536]{2,1,0:T(8,128)(2,1)S(1)}, bf16[8,128,1536]{2,1,0:T(8,128)(2,1)}, u32[]{:S(2)}) copy-start(bf16[8,128,1536]{2,1,0:T(8,128)(2,1)} %get-tuple-element.22) | copy-start | bytes 9437188
  80.7 3.9 %copy-start.16 = (f32[1024,512]{1,0:T(8,128)S(1)}, f32[1024,512]{1,0:T(8,128)}, u32[]{:S(2)}) copy-start(f32[1024,512]{1,0:T(8,128)} %copy-done.15) | copy-start | bytes 6291460
  80.7 3.9 %copy-start.21 = (f32[768]{0:T(1024)S(1)}, f32[768]{0:T(1024)}, u32[]{:S(2)}) copy-start(f32[768]{0:T(1024)} %param.23) | copy-start | bytes 9220
  80.7 3.9 %copy-start.23 = (f32[768]{0:T(1024)S(1)}, f32[768]{0:T(1024)}, u32[]{:S(2)}) copy-start(f32[768]{0:T(1024)} %param.22) | copy-start | bytes 9220
  91.8 3.0 %copy-start.12 = (f32[1024,384]{1,0:T(8,128)S(1)}, f32[1024,384]{1,0:T(8,128)}, u32[]{:S(2)}) copy-start(f32[1024,384]{1,0:T(8,128)} %get-tuple-element.56) | copy-start | bytes 4718596
  94.8 1.0 copy-start.6
  94.8 2.0 %copy-start.10 = (bf16[8,128,1536]{2,1,0:T(8,128)(2,1)S(1)}, bf16[8,128,1536]{2,1,0:T(8,128)(2,1)}, u32[]{:S(2)}) copy-start(bf16[8,128,1536]{2,1,0:T(8,128)(2,1)} %get-tuple-element.22) | copy-start | bytes 9437188
  96.8 1.1 copy-start.13
  97.9 1.5 copy-start.14
  99.4 1.1 copy-start.4
  100.6 1.1 copy-start.24
  104.2 63.8 %copy-start.7 = (bf16[1,128,768]{2,1,0:T(8,128)(2,1)S(1)}, bf16[1,128,768]{2,1,0:T(8,128)(2,1)}, u32[]{:S(2)}) copy-start(bf16[1,128,768]{2,1,0:T(8,128)(2,1)} %param.16) | copy-start | bytes 589828
  104.2 64.0 %copy-start.11 = (bf16[1,128,768]{2,1,0:T(8,128)(2,1)S(1)}, bf16[1,128,768]{2,1,0:T(8,128)(2,1)}, u32[]{:S(2)}) copy-start(bf16[1,128,768]{2,1,0:T(8,128)(2,1)} %param.17) | copy-start | bytes 589828
  104.2 64.0 %copy-start.18 = (f32[768]{0:T(1024)S(1)}, f32[768]{0:T(1024)}, u32[]{:S(2)}) copy-start(f32[768]{0:T(1024)} %param.31) | copy-start | bytes 9220
  104.2 64.0 %copy-start.19 = (f32[768]{0:T(1024)S(1)}, f32[768]{0:T(1024)}, u32[]{:S(2)}) copy-start(f32[768]{0:T(1024)} %param.27) | copy-start | bytes 9220
  167.9 4.3 %copy-start.1 = (bf16[8,192,1280]{2,1,0:T(8,128)(2,1)}, bf16[8,192,1280]{2,1,0:T(8,128)(2,1)S(1)}, u32[]{:S(2)}) copy-start(bf16[8,192,1280]{2,1,0:T(8,128)(2,1)S(1)} %get-tuple-element.29) | copy-start | bytes 11796484
  171.4 15.6 %copy-start.17 = (f32[768]{0:T(1024)}, f32[768]{0:T(1024)S(1)}, u32[]{:S(2)}) copy-start(f32[768]{0:T(1024)S(1)} %get-tuple-element.90) | copy-start | bytes 9220

commit v2 on v1

--- a/solution.py
+++ b/solution.py
@@ -555,19 +555,26 @@
     for k in (1, 2, 3, 0):
         block = ((chip + k) % CHIPS) * 2 + 1 - core
         go(push(y_ref.at[block], pair.at[k], pair_s.at[k], pair_r.at[k], ctx=sibling))
-    for piece in range(PIECES):
+    deep_sends = []
+
+    def send_piece(piece):
         rows = pl.ds(piece * part_rows, part_rows)
-        for k in range(1, DEPTH):
-            target = (depth + k) % DEPTH
-            go(
-                push(
-                    w_ref.at[target, rows],
-                    deep.at[k - 1, rows],
-                    zs.at[piece, k - 1],
-                    zr.at[piece, k - 1],
-                    fsdp=target,
-                )
+        copies = [
+            push(
+                w_ref.at[(depth + k) % DEPTH, rows],
+                deep.at[k - 1, rows],
+                zs.at[piece, k - 1],
+                zr.at[piece, k - 1],
+                fsdp=(depth + k) % DEPTH,
             )
+            for k in range(1, DEPTH)
+        ]
+        for copy in copies:
+            copy.start()
+        deep_sends.append(copies)
+
+    send_piece(0)
+    send_piece(1)
     for k in (1, 2, 3, 0):
         push(pair.at[k], pair.at[k], pair_s.at[k], pair_r.at[k], ctx=sibling).wait_recv()
         joint = y_ref[peer(k)].astype(jnp.float32) + pair[k].astype(jnp.float32)
@@ -599,6 +606,10 @@
             slot = deep.at[k - 1, rows]
             push(slot, slot, zs.at[piece, k - 1], zr.at[piece, k - 1], fsdp=depth).wait_recv()
             total = total + deep[k - 1, rows].astype(jnp.float32)
+        if piece + 2 < PIECES:
+            for copy in deep_sends[piece]:
+                copy.wait_send()
+            send_piece(piece + 2)
         w_all[me, rows] = total.astype(jnp.bfloat16)
         block = w_all.at[me, rows]
         for k in range(1, CHIPS):
@@ -623,7 +634,7 @@
         for k in range(CHIPS):
             block = w_all.at[((chip + CHIPS - k) % CHIPS) * 2 + 1 - core, rows]
             push(block, block, ss.at[piece, k], sr.at[piece, k], ctx=sibling).wait_recv()
-    for copy in sends:
+    for copy in sends + deep_sends[PIECES - 2] + deep_sends[PIECES - 1]:
         copy.wait_send()
 
 
@@ -741,6 +752,37 @@
     )(joined, d_mix, *tables, places[:, None], lowest[:, None], places[None, :])
 
 
+def spread_kernel(holders, units, grads_ref, fused_ref, up_ref, down_ref, attn_ref):
+    context, shard, _ = grads_ref.shape
+    width = holders * PAIR
+    ends = (3 * PAIR, 3 * PAIR + units, 3 * PAIR + 2 * units)
+    for owner in range(context):
+        own = slice(owner * units, (owner + 1) * units)
+        up_ref[:, own] = grads_ref[owner, :, ends[0] : ends[1]].astype(jnp.float32)
+        down_ref[:, own] = grads_ref[owner, :, ends[1] : ends[2]].astype(jnp.float32)
+        if owner < holders:
+            heads = slice(owner * PAIR, (owner + 1) * PAIR)
+            attn_ref[:, heads] = grads_ref[owner, :, ends[2] :].astype(jnp.float32)
+            for part in range(3):
+                target = slice(part * width + owner * PAIR, part * width + (owner + 1) * PAIR)
+                fused_ref[:, target] = grads_ref[
+                    owner, :, part * PAIR : (part + 1) * PAIR
+                ].astype(jnp.float32)
+
+
+def spread_grads(grads, holders, units):
+    context, shard, _ = grads.shape
+    width = holders * PAIR
+    shapes = ((shard, 3 * width), (shard, context * units), (shard, context * units), (shard, width))
+    return pl.pallas_call(
+        lambda *refs: spread_kernel(holders, units, *refs),
+        out_shape=tuple(jax.ShapeDtypeStruct(shape, jnp.float32) for shape in shapes),
+        in_specs=[VMEM_SPEC],
+        out_specs=(VMEM_SPEC,) * 4,
+        compiler_params=pltpu.CompilerParams(vmem_limit_bytes=32 * 1024 * 1024),
+    )(grads)
+
+
 def split_local(
     layer_input,
     cotangent,
@@ -771,28 +813,27 @@
     slot = jnp.minimum(me, holders - 1)
     holds = me < holders
 
-    own_joined = lax.dynamic_slice(
-        joined_weight.reshape(shard, 3, width), (0, 0, slot * PAIR), (shard, 3, PAIR)
-    ).reshape(shard, 3 * PAIR)
+    own_joined = jnp.concatenate(
+        [
+            lax.dynamic_slice(joined_weight, (0, part * width + slot * PAIR), (shard, PAIR))
+            for part in range(3)
+        ],
+        1,
+    )
     own_attn = lax.dynamic_slice(attn_weight, (slot * PAIR, 0), (PAIR, shard)).T
     own_up = lax.dynamic_slice(up_weight, (0, me * units), (shard, units))
     own_down = lax.dynamic_slice(down_weight, (me * units, 0), (units, shard)).T
     own_weights = jnp.concatenate(
-        [
-            jnp.where(holds, own_joined, 0),
-            own_up,
-            own_down,
-            jnp.where(holds, own_attn, 0),
-        ],
-        1,
-    )
+        [jnp.where(holds, own_joined, 0), jnp.where(holds, own_attn, 0)], 1
+    )
+    own_mlp = jnp.concatenate([own_up, own_down], 1)
+    mlp_all = lax.all_gather(own_mlp, "fsdp", axis=0, tiled=True)
     own_rows = jnp.concatenate([layer_input[0], cotangent[0]], 1)
     rows_all, weights_all = gather_all(own_rows, own_weights)
     rows_all = rows_all.reshape(length, 2 * width)
     weights_all = weights_all.reshape(width, -1)
     w_joined = weights_all[:, : 3 * PAIR]
-    w_up = weights_all[:, 3 * PAIR : 3 * PAIR + units]
-    w_out = weights_all[:, 3 * PAIR + units :]
+    w_attn = weights_all[:, 3 * PAIR :]
     hidden = rows_all[:, :width].astype(jnp.float32)
     grad_out = rows_all[:, width:]
     b_joined = jnp.where(
@@ -820,15 +861,18 @@
     norm_attn = (normal * attn_gain + attn_shift).astype(jnp.bfloat16)
     norm_mlp = (normal * mlp_gain + mlp_shift).astype(jnp.bfloat16)
     joined = jnp.dot(norm_attn, w_joined, preferred_element_type=jnp.float32) + b_joined
+    d_mix = jnp.dot(grad_out, w_attn, preferred_element_type=jnp.float32).astype(jnp.bfloat16)
+    mix_low, d_joined_low, joined_sums = attention(joined, d_mix, tables, places, lowest)
+    mlp_all, mix_low = lax.optimization_barrier((mlp_all, mix_low))
+    w_up = mlp_all[:, :units]
+    w_down = mlp_all[:, units:]
     upper = jnp.dot(norm_mlp, w_up, preferred_element_type=jnp.float32) + b_up
-    d_out = jnp.dot(grad_out, w_out, preferred_element_type=jnp.float32)
-    d_act = d_out[:, :units]
-    d_mix = d_out[:, units:].astype(jnp.bfloat16)
-    mix_low, d_joined_low, joined_sums = attention(joined, d_mix, tables, places, lowest)
+    d_act = jnp.dot(grad_out, w_down, preferred_element_type=jnp.float32)
     act, gelu_pull = jax.vjp(lambda argument: jax.nn.gelu(argument, approximate=False), upper)
     d_up = gelu_pull(d_act)[0]
     d_up_low = d_up.astype(jnp.bfloat16)
     outer = jnp.concatenate([act.astype(jnp.bfloat16), mix_low], 1)
+    w_out = jnp.concatenate([w_down, w_attn], 1)
     branches = lax.dot_general(outer, w_out, contract_cols, preferred_element_type=jnp.float32)
     d_norm_attn = lax.dot_general(
         d_joined_low, w_joined, contract_cols, preferred_element_type=jnp.float32
@@ -876,17 +920,7 @@
         - own_normal * jnp.mean(inner * own_normal, -1, keepdims=True)
     )
     input_grad = cotangent[0].astype(jnp.float32) + back
-    ends = (3 * PAIR, 3 * PAIR + units, 3 * PAIR + 2 * units)
-    dfused = (
-        grads[:holders, :, : ends[0]]
-        .reshape(holders, shard, 3, PAIR)
-        .transpose(1, 2, 0, 3)
-        .reshape(shard, 3 * width)
-        .astype(jnp.float32)
-    )
-    dup = grads[:, :, ends[0] : ends[1]].transpose(1, 0, 2).reshape(shard, -1).astype(jnp.float32)
-    ddown = grads[:, :, ends[1] : ends[2]].transpose(0, 2, 1).reshape(-1, shard).astype(jnp.float32)
-    dattn = grads[:holders, :, ends[2] :].transpose(0, 2, 1).reshape(width, shard)
+    dfused, dup, ddown, dattn = spread_grads(grads, holders, units)
     base = 4 * width
     fused_end = base + 3 * width
     out_end = fused_end + width
@@ -899,11 +933,11 @@
         small[3 * width : base],
         dfused,
         small[base:fused_end],
-        dattn.astype(jnp.float32),
+        dattn.T,
         small[fused_end:out_end],
         dup,
         small[out_end:],
-        ddown,
+        ddown.T,
         small[fused_end:out_end],
     )
 

time: 189 us -> 186 us (0.984)
  between operations: 1.93 us -> 15.3 us
  local copies, waits for them, and re-layouts: 24.7 us -> 13.8 us
  Pallas kernels: 116 us -> 110 us
  other arithmetic: 22 us -> 16.4 us
  matrix products: 23.4 us -> 28.4 us
    convert_element_type x5 -> x0, local copies, waits for them, and re-layouts: 11.2 us -> none  [the longest x3 7.87 us: split_local(): dfused = grads[:holders, :, :ends[0]].reshape(holders, shard, 3, PAIR).tr...]
    pallas_call x1, Pallas kernels: 40.2 us -> 30.9 us  [gather_all(): pl.pallas_call(gather_kernel, out_shape=(jax.ShapeDtypeStruct((2 * CHIPS,...]
    pallas_call x0 -> x1, Pallas kernels: none -> 3.25 us  [spread_grads(): pl.pallas_call(lambda *refs: spread_kernel(holders, units, *refs), out_sh...]
    dot_general x1, matrix products: 1.01 us -> 4.14 us  [split_local(): lax.dot_general(d_joined_low, w_joined, contract_cols, preferred_element_...]
    reshape x1 -> x0, local copies, waits for them, and re-layouts: 3.11 us -> none  [split_local(): joined_weight.reshape(shard, 3, width)]
    convert_element_type x3 -> x0, other arithmetic: 2.42 us -> none  [the longest x1 1.33 us: split_local(): dfused = grads[:holders, :, :ends[0]].reshape(holders, shard, 3, PAIR).tr...]
    unnamed x2 -> x1, other arithmetic: 2.12 us -> 0.01 us
    unnamed x58 -> x83, local copies, waits for them, and re-layouts: 5.75 us -> 6.97 us
  transfers between devices with their start and end apart: 0 -> 1, of which waited for: 0 -> 0; matrix products, arithmetic and copies ran while one was open for 0% -> 16% of each run, Pallas kernels for 0% -> 23%
where the time goes in v2:
time: 186 us; the launch traced here: 184 us
  Pallas kernels  110 us (59%)
  matrix products  28.4 us (15%)
  other arithmetic  16.4 us (9%)
  between operations  15.3 us (8%)
  local copies, waits for them, and re-layouts  13.8 us (7%)
    pallas_call x1, Pallas kernels, reduce_all(): pl.pallas_call(reduce_kernel, out_shape=(jax.ShapeDtypeStruct((rows, colu...  64.2 us
    pallas_call x1, Pallas kernels, gather_all(): pl.pallas_call(gather_kernel, out_shape=(jax.ShapeDtypeStruct((2 * CHIPS,...  30.9 us
    pallas_call x1, Pallas kernels, attention(): pl.pallas_call(attention_kernel, out_shape=(jax.ShapeDtypeStruct((length,...  11.5 us
    unnamed x83, local copies, waits for them, and re-layouts  6.97 us
    dot_general x1, matrix products, split_local(): upper = jnp.dot(norm_mlp, w_up, preferred_element_type=jnp.float32) + b_up  6.88 us
    dot_general x1, matrix products, split_local(): lax.dot_general(d_joined_low, w_joined, contract_cols, preferred_element_...  4.14 us
    dot_general x1, matrix products, split_local(): jnp.dot(norm_attn, w_joined, preferred_element_type=jnp.float32) + b_joined  3.78 us
  transfers between devices with their start and end apart: 1, of which 0 were waited for; matrix products, arithmetic and copies ran while one was open for 16% of the time, Pallas kernels for 23%

profile of v2, /device:TPU:0, one launch (start us, length us, event | category | flops | bytes accessed | tf_op | source)
XLA Modules:
  0.0 183.8 jit_solution(1139949557550091698)
XLA Ops:
  7.2 0.0 copy-start
  7.2 0.0 all-gather.2.cloned.1.call-start
  7.3 1.2 copy-done
  8.5 0.9 dynamic-slice_bitcast_fusion
  9.4 0.7 pad_maximum_fusion.6
  10.1 0.0 all-gather.2.cloned.1.call-update
  10.2 0.5 compare_and_fusion
  10.7 0.5 broadcast_compare_fusion.1
  11.2 0.5 fusion.69
  11.8 0.8 select_bitcast_fusion
  12.6 0.9 constant_dynamic-slice_fusion.3
  13.5 0.7 pad_maximum_fusion.7.b_ref
  14.2 0.8 pad_maximum_fusion.5.a_ref
  15.0 30.9 %shard_map.263 = (bf16[8,128,1536]{2,1,0:T(8,128)(2,1)}, bf16[4,192,512]{2,1,0:T(8,128)(2,1)}) custom-call(bf16[128,1536]{1,0:T(8,128)(2,1)} %pad_maximum_fusion.5.a_ref, bf16[192,512]{1,0:T(8,128)(2,1)} %pad_maximum_fusion.7.b_ref), custom_call_target="tpu_custom_call" | custom-call | tf_op jit(solution)/shard_map/pallas_call | solution.py:511
  45.9 1.8 convert_reduce_fusion
  47.8 0.0 copy-start.30
  47.8 2.0 %convolution_convert_fusion.4.dmix_ref = bf16[1024,128]{1,0:T(8,128)(2,1)S(1)} fusion(bf16[1024,1536]{1,0:T(8,128)(2,1)} %bitcast.56, bf16[768,512]{1,0:T(8,128)(2,1)} %bitcast.68), kind=kOutput, calls=%fused_computation.41 | convolution fusion | flops 201457664 | bytes 2031616 | tf_op jit(solution)/shard_map/dot_general | solution.py:864
  49.8 0.0 copy-start.34
  49.8 0.6 fusion.12
  50.5 0.1 select_reduce_fusion
  50.6 0.2 copy.31
  51.5 0.1 compare_select_fusion
  51.6 0.0 copy-start.26
  51.6 0.0 copy-start.27
  51.7 3.8 %convolution_add_fusion.1.joined_ref = f32[1024,384]{1,0:T(8,128)} fusion(f32[384]{0:T(512)S(1)} %select_bitcast_fusion.1, bf16[768,512]{1,0:T(8,128)(2,1)} %bitcast.69, f32[768]{0:T(1024)S(1)} %copy-done.31, f32[768]{0:T(1024)S(1)} %copy-done.34, f32[1024]{0:T(1024)S(1)} %add_rsqrt_fusion, f32[1024]{0:T(1024)S(1)} %broadcast_multiply_fusion.1, ...), kind=kOutput, calls=%fused_computation.37 | convolution fusion | flops 609091584 | bytes 3751424 | tf_op jit(solution)/shard_map/dot_general | solution.py:863
  55.5 3.0 %fusion.28 = (f32[1024,128]{1,0:T(8,128)S(1)}, f32[1024,128]{1,0:T(8,128)S(1)}, f32[1024,128]{1,0:T(8,128)}) fusion(f32[128]{0:T(128)S(1)} %copy-done.29, f32[1024]{0:T(1024)S(1)} %get-tuple-element.67, pred[128]{0:T(512)(128)(4,1)S(1)} %copy-done.26, pred[128]{0:T(512)(128)(4,1)S(1)} %copy-done.27, pred[128]{0:T(512)(128)(4,1)S(1)} %copy-done.28), kind=kLoop, calls=%fused_computation.53 | loop fusion | flops 655360 | bytes 1577856 | tf_op jit(solution)/shard_map/jit(_where)/select_n | solution.py:857
  58.5 0.5 iota_compare_fusion.1
  59.0 1.6 slice.96
  60.6 1.3 dynamic_slice.31
  62.0 1.0 copy-done.1
  63.0 1.4 copy-done.2
  64.4 11.5 %shard_map.264 = (bf16[1024,128]{1,0:T(8,128)(2,1)S(1)}, bf16[1024,384]{1,0:T(8,128)(2,1)S(1)}, f32[1,384]{1,0:T(1,128)S(1)}) custom-call(f32[1024,384]{1,0:T(8,128)S(1)} %copy-done.2, bf16[1024,128]{1,0:T(8,128)(2,1)S(1)} %convolution_convert_fusion.4.dmix_ref, f32[1024,128]{1,0:T(8,128)S(1)} %copy-done.1, f32[1024,128]{1,0:T(8,128)S(1)} %get-tuple-element.64.down_ref, ...), custom_call_target="tpu_custom_call" | custom-call | tf_op jit(solution)/shard_map/pallas_call | solution.py:741
  76.0 0.0 copy-start.3
  76.0 0.9 copy-done.3
  76.8 0.7 copy-done.6
  77.6 0.7 broadcast_select_fusion.1
  78.3 1.0 convert_reduce_fusion.2
  79.3 1.0 convert_reduce_fusion.1
  80.3 1.1 fusion.49
  81.5 0.0 copy-start.35
  81.5 4.1 %fusion.36 = f32[1024,768]{1,0:T(8,128)} fusion(bf16[1024,384]{1,0:T(8,128)(2,1)} %copy-done.3, bf16[768,512]{1,0:T(8,128)(2,1)} %bitcast.71), kind=kOutput, calls=%fused_computation.66 | convolution fusion | flops 603979776 | bytes 4521984 | tf_op jit(solution)/shard_map/dot_general | solution.py:877
  85.7 0.0 copy-start.24
  85.7 0.0 copy-start.33
  85.7 2.3 %convolution_convert_fusion.3 = bf16[768,384]{1,0:T(8,128)(2,1)} fusion(bf16[1024,384]{1,0:T(8,128)(2,1)S(1)} %copy-done.4, f32[768]{0:T(1024)S(1)} %copy-done.32, f32[768]{0:T(1024)S(1)} %copy-done.35, f32[1024]{0:T(1024)S(1)} %add_rsqrt_fusion, f32[1024]{0:T(1024)S(1)} %broadcast_multiply_fusion.1, bf16[1024,1536]{1,0:T(8,128)(2,1)S(1)} %bitcast.61), kind=kOutput, calls=%fused_computation.40 | convolution fusion | flops 608993280 | bytes 2965504 | tf_op jit(solution)/shard_map/dot_general | solution.py:885
  88.1 6.9 %multiply_convert_fusion = (bf16[1024,384]{1,0:T(8,128)(2,1)}, f32[1024,384]{1,0:T(8,128)S(1)}, f32[1024,384]{1,0:T(8,128)S(1)}) fusion(f32[384]{0:T(512)S(1)} %copy-done.24, bf16[768,768]{1,0:T(8,128)(2,1)} %all-gather.2.cloned.1.call-done, f32[768]{0:T(1024)S(1)} %copy-done.33, f32[768]{0:T(1024)S(1)} %copy-done.36, f32[1024]{0:T(1024)S(1)} %add_rsqrt_fusion, ...), kind=kOutput, calls=%fused_computation.22 | convolution fusion | flops 634650624 | bytes 6110720 | tf_op jit(solution)/shard_map/dot_general | solution.py:869
  94.9 1.4 fusion.80
  96.4 2.1 %convolution_convert_fusion.2 = bf16[768,384]{1,0:T(8,128)(2,1)} fusion(bf16[1024,384]{1,0:T(8,128)(2,1)S(1)} %get-tuple-element.70, f32[768]{0:T(1024)S(1)} %copy-done.33, f32[768]{0:T(1024)S(1)} %copy-done.36, f32[1024]{0:T(1024)S(1)} %add_rsqrt_fusion, f32[1024]{0:T(1024)S(1)} %broadcast_multiply_fusion.1, bf16[1024,1536]{1,0:T(8,128)(2,1)S(1)} %bitcast.63), kind=kOutput, calls=%fused_computation.39 | convolution fusion | flops 608993280 | bytes 2965504 | tf_op jit(solution)/shard_map/dot_general | solution.py:886
  98.5 1.9 %fusion.11 = (f32[768]{0:T(1024)S(1)}, f32[768]{0:T(1024)S(1)}, f32[768]{0:T(1024)S(1)}, f32[768]{0:T(1024)S(1)}, bf16[1024,768]{1,0:T(8,128)(2,1)S(1)}) fusion(f32[1024]{0:T(1024)S(1)} %add_rsqrt_fusion, f32[1024]{0:T(1024)S(1)} %broadcast_multiply_fusion.1, bf16[1024,1536]{1,0:T(8,128)(2,1)S(1)} %bitcast.64, f32[1024,768]{1,0:T(8,128)S(1)} %copy-done.13, ...), kind=kOutput, calls=%fused_computation.13 | convolution fusion | flops 614200320 | bytes 7696384 | tf_op jit(solution)/shard_map/dot_general | solution.py:880
  100.5 0.1 broadcast_select_fusion
  100.7 0.0 copy-start.19
  100.7 2.7 %convolution_convert_fusion.1 = bf16[768,512]{1,0:T(8,128)(2,1)S(1)} fusion(bf16[1024,1536]{1,0:T(8,128)(2,1)} %bitcast.59, bf16[1024,128]{1,0:T(8,128)(2,1)S(1)} %copy-done.7, bf16[1024,384]{1,0:T(8,128)(2,1)} %get-tuple-element.48), kind=kOutput, calls=%fused_computation.38 | convolution fusion | flops 807796736 | bytes 3407872 | tf_op jit(solution)/shard_map/dot_general | solution.py:887
  103.4 1.0 convolution_convert_fusion
  104.5 0.3 pad_maximum_fusion.y_ref
  104.8 0.8 copy-done.17
  105.5 0.2 copy-done.18
  105.7 0.1 pad_maximum_fusion.1.w_ref
  105.9 64.2 %shard_map.265 = (f32[128,1536]{1,0:T(8,128)S(1)}, bf16[8,192,1280]{2,1,0:T(8,128)(2,1)S(1)}, f32[72,128]{1,0:T(8,128)S(1)}) custom-call(bf16[8,128,1536]{2,1,0:T(8,128)(2,1)S(1)} %pad_maximum_fusion.y_ref, bf16[4,192,1280]{2,1,0:T(8,128)(2,1)S(1)} %pad_maximum_fusion.1.w_ref, f32[72,128]{1,0:T(8,128)S(1)} %bitcast.53), custom_call_target="tpu_custom_call" | custom-call | tf_op jit(solution)/shard_map/pallas_call | solution.py:644
  170.1 0.6 slice_bitcast_fusion.2
  170.7 0.6 slice_bitcast_fusion
  171.3 0.6 slice_bitcast_fusion.1
  171.9 3.2 %shard_map.266 = (f32[192,2304]{1,0:T(8,128)}, f32[192,3072]{1,0:T(8,128)}, f32[192,3072]{1,0:T(8,128)}, f32[192,768]{1,0:T(8,128)}) custom-call(bf16[8,192,1280]{2,1,0:T(8,128)(2,1)S(1)} %get-tuple-element.37.refs_0_), custom_call_target="tpu_custom_call" | custom-call | tf_op jit(solution)/shard_map/pallas_call | solution.py:777
  175.2 0.2 slice_reduce_fusion
  175.4 1.0 fusion.50
  176.4 0.6 copy.41
  (86 shorter events, 0.3 us)
Async XLA Ops:
  7.2 1.3 copy-start
  7.2 7.0 %copy-start.8 = (bf16[1,128,768]{2,1,0:T(8,128)(2,1)S(1)}, bf16[1,128,768]{2,1,0:T(8,128)(2,1)}, u32[]{:S(2)}) copy-start(bf16[1,128,768]{2,1,0:T(8,128)(2,1)} %param.16) | copy-start | bytes 589828
  7.2 7.0 %copy-start.14 = (bf16[1,128,768]{2,1,0:T(8,128)(2,1)S(1)}, bf16[1,128,768]{2,1,0:T(8,128)(2,1)}, u32[]{:S(2)}) copy-start(bf16[1,128,768]{2,1,0:T(8,128)(2,1)} %param.17) | copy-start | bytes 589828
  7.2 80.8 %all-gather.2.cloned.1.call-start = ((), (), s32[]{:S(2)}) async-start(), calls=%async_computation | async-start | bytes 1474560 | tf_op jit(solution)/shard_map/all_gather | solution.py:830
  45.9 3.9 %copy-start.10 = (bf16[8,128,1536]{2,1,0:T(8,128)(2,1)S(1)}, bf16[8,128,1536]{2,1,0:T(8,128)(2,1)}, u32[]{:S(2)}) copy-start(bf16[8,128,1536]{2,1,0:T(8,128)(2,1)} %get-tuple-element.28) | copy-start | bytes 9437188
  47.8 2.7 %copy-start.21 = (f32[2304]{0:T(1024)S(1)}, f32[2304]{0:T(1024)}, u32[]{:S(2)}) copy-start(f32[2304]{0:T(1024)} %param.25) | copy-start | bytes 27652
  47.8 2.7 %copy-start.30 = (s32[16]{0:T(128)S(1)}, s32[16]{0:T(128)}, u32[]{:S(2)}) copy-start(s32[16]{0:T(128)} %param.18) | copy-start | bytes 196
  49.8 1.8 copy-start.31
  49.8 1.8 copy-start.34
  51.6 3.8 %copy-start.26 = (pred[128]{0:T(512)(128)(4,1)S(1)}, pred[128]{0:T(512)(128)(4,1)}, u32[]{:S(2)}) copy-start(pred[128]{0:T(512)(128)(4,1)} %get-tuple-element.71) | copy-start | bytes 388
  51.6 3.8 %copy-start.27 = (pred[128]{0:T(512)(128)(4,1)S(1)}, pred[128]{0:T(512)(128)(4,1)}, u32[]{:S(2)}) copy-start(pred[128]{0:T(512)(128)(4,1)} %get-tuple-element.72) | copy-start | bytes 388
  51.7 3.8 %copy-start.28 = (pred[128]{0:T(512)(128)(4,1)S(1)}, pred[128]{0:T(512)(128)(4,1)}, u32[]{:S(2)}) copy-start(pred[128]{0:T(512)(128)(4,1)} %broadcast_compare_fusion.1) | copy-start | bytes 388
  51.7 3.8 %copy-start.29 = (f32[128]{0:T(128)S(1)}, f32[128]{0:T(128)}, u32[]{:S(2)}) copy-start(f32[128]{0:T(128)} %fusion.69) | copy-start | bytes 1540
  62.0 1.0 copy-start.1
  63.0 1.4 copy-start.2
  76.0 0.9 copy-start.3
  76.8 0.7 copy-start.6
  81.5 4.2 %copy-start.4 = (bf16[1024,384]{1,0:T(8,128)(2,1)S(1)}, bf16[1024,384]{1,0:T(8,128)(2,1)}, u32[]{:S(2)}) copy-start(bf16[1024,384]{1,0:T(8,128)(2,1)} %copy-done.3) | copy-start | bytes 2359300
  81.5 4.2 %copy-start.11 = (bf16[8,128,1536]{2,1,0:T(8,128)(2,1)S(1)}, bf16[8,128,1536]{2,1,0:T(8,128)(2,1)}, u32[]{:S(2)}) copy-start(bf16[8,128,1536]{2,1,0:T(8,128)(2,1)} %get-tuple-element.28) | copy-start | bytes 9437188
  81.5 4.2 %copy-start.32 = (f32[768]{0:T(1024)S(1)}, f32[768]{0:T(1024)}, u32[]{:S(2)}) copy-start(f32[768]{0:T(1024)} %param.21) | copy-start | bytes 9220
  81.5 4.2 %copy-start.35 = (f32[768]{0:T(1024)S(1)}, f32[768]{0:T(1024)}, u32[]{:S(2)}) copy-start(f32[768]{0:T(1024)} %param.20) | copy-start | bytes 9220
  85.7 2.4 %copy-start.24 = (f32[384]{0:T(512)S(1)}, f32[384]{0:T(512)}, u32[]{:S(2)}) copy-start(f32[384]{0:T(512)} %dynamic_slice.31) | copy-start | bytes 4612
  85.7 2.4 %copy-start.33 = (f32[768]{0:T(1024)S(1)}, f32[768]{0:T(1024)}, u32[]{:S(2)}) copy-start(f32[768]{0:T(1024)} %param.23) | copy-start | bytes 9220
  85.7 2.4 %copy-start.36 = (f32[768]{0:T(1024)S(1)}, f32[768]{0:T(1024)}, u32[]{:S(2)}) copy-start(f32[768]{0:T(1024)} %param.22) | copy-start | bytes 9220
  88.0 6.9 %copy-start.12 = (bf16[8,128,1536]{2,1,0:T(8,128)(2,1)S(1)}, bf16[8,128,1536]{2,1,0:T(8,128)(2,1)}, u32[]{:S(2)}) copy-start(bf16[8,128,1536]{2,1,0:T(8,128)(2,1)} %get-tuple-element.28) | copy-start | bytes 9437188
  88.1 6.9 %copy-start.16 = (bf16[768,768]{1,0:T(8,128)(2,1)S(1)}, bf16[768,768]{1,0:T(8,128)(2,1)}, u32[]{:S(2)}) copy-start(bf16[768,768]{1,0:T(8,128)(2,1)} %all-gather.2.cloned.1.call-done) | copy-start | bytes 3538948
  96.4 2.1 %copy-start.13 = (f32[1024,768]{1,0:T(8,128)S(1)}, f32[1024,768]{1,0:T(8,128)}, u32[]{:S(2)}) copy-start(f32[1024,768]{1,0:T(8,128)} %fusion.36) | copy-start | bytes 9437188
  98.5 2.0 %copy-start.25 = (pred[8]{0:T(512)(128)(4,1)S(1)}, pred[8]{0:T(512)(128)(4,1)}, u32[]{:S(2)}) copy-start(pred[8]{0:T(512)(128)(4,1)} %iota_compare_fusion.1) | copy-start | bytes 28
  98.5 2.0 %copy-start.5 = (f32[9216]{0:T(1024)S(1)}, f32[9216]{0:T(1024)}, u32[]{:S(2)}) copy-start(f32[9216]{0:T(1024)} %custom-call) | copy-start | bytes 110596
  98.5 2.1 %copy-start.7 = (bf16[1024,128]{1,0:T(8,128)(2,1)S(1)}, bf16[1024,128]{1,0:T(8,128)(2,1)}, u32[]{:S(2)}) copy-start(bf16[1024,128]{1,0:T(8,128)(2,1)} %copy-done.6) | copy-start | bytes 786436
  100.6 2.8 %slice-start = ((bf16[768,768]{1,0:T(8,128)(2,1)}), bf16[768,384]{1,0:T(8,128)(2,1)S(1)}, s32[]{:S(2)}) async-start(bf16[768,768]{1,0:T(8,128)(2,1)} %all-gather.2.cloned.1.call-done), calls=%async_computation.1 | async-start | bytes 1179648 | tf_op jit(solution)/shard_map/slice | solution.py:868
  100.7 2.8 %copy-start.19 = (bf16[768,128]{1,0:T(8,128)(2,1)S(1)}, bf16[768,128]{1,0:T(8,128)(2,1)}, u32[]{:S(2)}) copy-start(bf16[768,128]{1,0:T(8,128)(2,1)} %slice.96) | copy-start | bytes 589828
  100.7 2.8 %copy-start.37 = (bf16[1024,384]{1,0:T(8,128)(2,1)S(1)}, bf16[1024,384]{1,0:T(8,128)(2,1)}, u32[]{:S(2)}) copy-start(bf16[1024,384]{1,0:T(8,128)(2,1)} %get-tuple-element.48) | copy-start | bytes 2359300
  104.5 1.1 copy-start.17
  104.5 1.2 copy-start.18
  170.7 5.7 %copy-start.20 = (f32[768]{0:T(1024)}, f32[768]{0:T(1024)S(1)}, u32[]{:S(2)}) copy-start(f32[768]{0:T(1024)S(1)} %get-tuple-element.102) | copy-start | bytes 9220
  171.9 3.3 %copy-start.9 = (bf16[1,128,768]{2,1,0:T(8,128)(2,1)S(1)}, bf16[1,128,768]{2,1,0:T(8,128)(2,1)}, u32[]{:S(2)}) copy-start(bf16[1,128,768]{2,1,0:T(8,128)(2,1)} %param.16) | copy-start | bytes 589828
  171.9 3.5 %copy-start.15 = (bf16[1,128,768]{2,1,0:T(8,128)(2,1)S(1)}, bf16[1,128,768]{2,1,0:T(8,128)(2,1)}, u32[]{:S(2)}) copy-start(bf16[1,128,768]{2,1,0:T(8,128)(2,1)} %param.17) | copy-start | bytes 589828
  171.9 3.5 %copy-start.22 = (f32[768]{0:T(1024)S(1)}, f32[768]{0:T(1024)}, u32[]{:S(2)}) copy-start(f32[768]{0:T(1024)} %param.31) | copy-start | bytes 9220
  171.9 3.5 %copy-start.23 = (f32[768]{0:T(1024)S(1)}, f32[768]{0:T(1024)}, u32[]{:S(2)}) copy-start(f32[768]{0:T(1024)} %param.27) | copy-start | bytes 9220
Sparse Core Ops, SparseCore 0:
  10.3 47.9 all-gather.1
